TPU v7x, 256 devices: a whole 4x4x8 slice. The times are simulated.
256 devices in a mesh: items: 128 (over z, x, y_hi, core), rep: 2 (over y_lo).
Axes of the slice: x: 4, y: 4 (y_hi: 2, y_lo: 2; y = y_hi * 2 + y_lo), z: 8, core: 2. Of those that a mesh axis runs over, the one named last changes fastest.
Arguments:
- teacher_queries: bfloat16 [262144, 1024], P(('items', 'rep')), may hold values from -6 to 6
- teacher_items: bfloat16 [65536, 1024], P('items'), may hold values from -6 to 6
- student_queries: bfloat16 [262144, 128], P(('items', 'rep')), may hold values from -6 to 6
- student_items: bfloat16 [65536, 128], P('items'), may hold values from -6 to 6
- block_mask: int32 [4096, 7], P(('items', 'rep')), may hold values from 0 to 1, as said below
- pass_index: int32 [262144], P(('items', 'rep')), may hold values from 0 to 3
- teacher_norms: float32 [4, 262144], P(None, ('items', 'rep')), may hold values from 8 to 10
- student_norms: float32 [4, 262144], P(None, ('items', 'rep')), may hold values from 8 to 10
Outputs:
- query_grad: float32 [262144, 128], P(('items', 'rep'))
- item_grad: float32 [65536, 128], P(('items', 'rep'))
Inputs may be any that keep to these rules, and one draw needn't show every extreme that they name: block_mask[b, o] is 1 where the requests of block b visit the span at offset o - 3 from their own span, else 0; a block visits at most 5 of the 7 offsets.
All inputs are finite; a program needn't handle non-finite values.
Results may differ from a plain program's by a relative error of at most 0.0026.
Values may be sent and summed in bfloat16 or wider, within the bound.
No kernel may reach another device: no remote copies, remote signals or barrier semaphores. Data moves between devices by JAX's collectives and lax.ppermute only.
A program may use at most 64 MiB of HBM per device.

v0:
```python
import math

import jax
import jax.numpy as jnp
from jax import lax
from jax.sharding import PartitionSpec as P

logit_cap = 10.0
score_gain = 3.0
loss_weight = 8.0


def from_behind(block, axis, distance):
    devices = range(lax.axis_size(axis))
    route = [((i - distance) % len(devices), i) for i in devices]
    return lax.ppermute(block, axis, route)


def pair_gradient(t_raw, s_raw, z_teacher, z_student, weight, teacher_scale, student_scale):
    teacher = logit_cap * jnp.tanh(t_raw * (teacher_scale / logit_cap))
    student = logit_cap * jnp.tanh(s_raw * (student_scale / logit_cap))
    slope = 1.0 - (student / logit_cap) ** 2
    diff = jnp.exp(student - z_student[:, None]) - jnp.exp(teacher - z_teacher[:, None])
    grads = loss_weight * student_scale * weight[:, None] * diff * slope
    return grads.astype(jnp.bfloat16)


def contract_rows(left, right):
    return lax.dot_general(
        left, right, (((1,), (1,)), ((), ())), preferred_element_type=jnp.float32
    )


def contract_cols(left, right):
    return lax.dot_general(
        left, right, (((0,), (0,)), ((), ())), preferred_element_type=jnp.float32
    )


def shards(
    teacher_queries,
    teacher_items,
    student_queries,
    student_items,
    block_mask,
    pass_index,
    teacher_norms,
    student_norms,
):
    rows = teacher_queries.shape[0]
    blocks = block_mask.shape[0]
    block_rows = rows // blocks
    visits = block_mask.shape[1]
    reach = visits // 2
    teacher_scale = score_gain / math.sqrt(teacher_queries.shape[1])
    student_scale = score_gain / math.sqrt(student_queries.shape[1])
    passes = jnp.arange(teacher_norms.shape[0], dtype=jnp.int32)
    picked = (pass_index[None, :] == passes[:, None]).astype(jnp.float32)
    z_teacher = jnp.sum(teacher_norms * picked, axis=0)
    z_student = jnp.sum(student_norms * picked, axis=0)
    weights = jnp.broadcast_to(
        block_mask.astype(jnp.float32)[:, None, :], (blocks, block_rows, visits)
    ).reshape(rows, visits)

    def scores(q_teacher, q_student, zt_rows, zs_rows, weight, e_teacher, e_student):
        t_raw = contract_rows(q_teacher, e_teacher)
        s_raw = contract_rows(q_student, e_student)
        return pair_gradient(t_raw, s_raw, zt_rows, zs_rows, weight, teacher_scale, student_scale)

    def visit(q_teacher, q_student, zt_rows, zs_rows, weight, e_teacher, e_student):
        return scores(q_teacher, q_student, zt_rows, zs_rows, weight, e_teacher, e_student)

    own_grad = visit(
        teacher_queries,
        student_queries,
        z_teacher,
        z_student,
        weights[:, reach],
        teacher_items,
        student_items,
    )
    query_grad = jnp.dot(own_grad, student_items, preferred_element_type=jnp.float32)
    item_total = contract_cols(own_grad, student_queries)
    current = (teacher_items, student_items)
    terms_ahead = []
    for step in range(reach):
        current = from_behind((current[0], current[1]), "items", -1)
        grad_pair = visit(
            teacher_queries,
            student_queries,
            z_teacher,
            z_student,
            weights[:, reach + step + 1],
            current[0],
            current[1],
        )
        query_grad = query_grad + jnp.dot(grad_pair, current[1], preferred_element_type=jnp.float32)
        terms_ahead.append(contract_cols(grad_pair, student_queries))
    current = (teacher_items, student_items)
    terms_behind = []
    for step in range(reach):
        current = from_behind((current[0], current[1]), "items", 1)
        grad_pair = visit(
            teacher_queries,
            student_queries,
            z_teacher,
            z_student,
            weights[:, reach - step - 1],
            current[0],
            current[1],
        )
        query_grad = query_grad + jnp.dot(grad_pair, current[1], preferred_element_type=jnp.float32)
        terms_behind.append(contract_cols(grad_pair, student_queries))
    carried = terms_ahead[reach - 1]
    for level in range(reach - 2, -2, -1):
        carried = from_behind(carried, "items", 1)
        if level >= 0:
            carried = carried + terms_ahead[level]
    item_total = item_total + carried
    carried = terms_behind[reach - 1]
    for level in range(reach - 2, -2, -1):
        carried = from_behind(carried, "items", -1)
        if level >= 0:
            carried = carried + terms_behind[level]
    item_total = item_total + carried
    item_grad = lax.psum_scatter(item_total, "rep", scatter_dimension=0, tiled=True)
    return (query_grad, item_grad)


def solution(mesh):
    return jax.shard_map(
        shards,
        mesh=mesh,
        in_specs=(
            P(("items", "rep"), None),
            P("items", None),
            P(("items", "rep"), None),
            P("items", None),
            P(("items", "rep"), None),
            P(("items", "rep")),
            P(None, ("items", "rep")),
            P(None, ("items", "rep")),
        ),
        out_specs=(P(("items", "rep"), None), P(("items", "rep"), None)),
        check_vma=False,
    )
```

profile of v0, /device:TPU:1, one launch (start us, length us, event | category | flops | bytes accessed | tf_op | source)
XLA Modules:
  0.0 167.1 jit_solution(8317292167906412205)
XLA Ops:
  7.2 4.4 %collective-permute-start.6 = (bf16[512,128]{1,0:T(8,128)(2,1)}, bf16[512,128]{1,0:T(8,128)(2,1)S(1)}, u32[]{:S(2)}, u32[]{:S(2)}) collective-permute-start(bf16[512,128]{1,0:T(8,128)(2,1)} %param.11), channel_id=1, source_target_pairs={{254,0},{0,2},{2,4},{4,6},{6,8},{8,10},{10,12},{12,14},{14,16},{16... | collective-permute-start | bytes 393224 | tf_op jit(solution)/shard_map/ppermute | solution.py:16
  11.6 3.2 %collective-permute-start.7 = (bf16[512,1024]{1,0:T(8,128)(2,1)}, bf16[512,1024]{1,0:T(8,128)(2,1)}, u32[]{:S(2)}, u32[]{:S(2)}) collective-permute-start(bf16[512,1024]{1,0:T(8,128)(2,1)} %param.9), channel_id=1, source_target_pairs={{254,0},{0,2},{2,4},{4,6},{6,8},{8,10},{10,12},{12,14},{14,16},{16... | collective-permute-start | bytes 3145736 | tf_op jit(solution)/shard_map/ppermute | solution.py:16
  14.9 4.2 %collective-permute-start.1 = (bf16[512,1024]{1,0:T(8,128)(2,1)}, bf16[512,1024]{1,0:T(8,128)(2,1)}, u32[]{:S(2)}, u32[]{:S(2)}) collective-permute-start(bf16[512,1024]{1,0:T(8,128)(2,1)} %param.9), channel_id=1, source_target_pairs={{2,0},{4,2},{6,4},{8,6},{10,8},{12,10},{14,12},{16,14},{18,16},{20... | collective-permute-start | bytes 3145736 | tf_op jit(solution)/shard_map/ppermute | solution.py:16
  19.0 0.7 convert_element_type.25
  20.0 2.6 %fusion.1 = f32[1024,512]{1,0:T(8,128)S(1)} fusion(bf16[1024,1024]{1,0:T(8,128)(2,1)S(1)} %copy-done, bf16[512,1024]{1,0:T(8,128)(2,1)} %param.9), kind=kOutput, calls=%fused_computation.26 | convolution fusion | flops 1073741824 | bytes 5242880 | tf_op jit(solution)/shard_map/dot_general | solution.py:29
  22.6 1.6 multiply_convert_fusion.6
  24.2 0.4 fusion.2
  24.7 0.5 fusion.10
  25.2 7.5 %collective-permute-start.2 = (bf16[512,128]{1,0:T(8,128)(2,1)S(1)}, bf16[512,128]{1,0:T(8,128)(2,1)S(1)}, u32[]{:S(2)}, u32[]{:S(2)}) collective-permute-start(bf16[512,128]{1,0:T(8,128)(2,1)S(1)} %collective-permute-done), channel_id=1, source_target_pairs={{2,0},{4,2},{6,4},{8,6},{10,8},{12,10},{14,12},{16,14},{18,16},{20... | collective-permute-start | bytes 393224 | tf_op jit(solution)/shard_map/ppermute | solution.py:16
  33.2 0.4 fusion.6
  33.7 7.8 %collective-permute-done.8 = bf16[512,128]{1,0:T(8,128)(2,1)S(1)} collective-permute-done((bf16[512,128]{1,0:T(8,128)(2,1)S(1)}, bf16[512,128]{1,0:T(8,128)(2,1)S(1)}, u32[]{:S(2)}, u32[]{:S(2)}) %collective-permute-start.8) | collective-permute-done | bytes 131104 | tf_op jit(solution)/shard_map/ppermute | solution.py:16
  41.5 4.0 %collective-permute-start.10 = (bf16[512,128]{1,0:T(8,128)(2,1)S(1)}, bf16[512,128]{1,0:T(8,128)(2,1)S(1)}, u32[]{:S(2)}, u32[]{:S(2)}) collective-permute-start(bf16[512,128]{1,0:T(8,128)(2,1)S(1)} %collective-permute-done.8), channel_id=1, source_target_pairs={{254,0},{0,2},{2,4},{4,6},{6,8},{8,10},{10,12},{12,14},{14,16},{16... | collective-permute-start | bytes 393224 | tf_op jit(solution)/shard_map/ppermute | solution.py:16
  45.5 0.8 collective-permute-done.2
  46.2 0.4 fusion.4
  46.7 0.4 fusion.8
  47.1 6.4 %collective-permute-done.4 = bf16[512,128]{1,0:T(8,128)(2,1)S(1)} collective-permute-done((bf16[512,128]{1,0:T(8,128)(2,1)S(1)}, bf16[512,128]{1,0:T(8,128)(2,1)S(1)}, u32[]{:S(2)}, u32[]{:S(2)}) %collective-permute-start.4) | collective-permute-done | bytes 131104 | tf_op jit(solution)/shard_map/ppermute | solution.py:16
  54.5 0.5 collective-permute-start.3
  55.0 3.7 %multiply_convert_fusion.5 = bf16[1024,512]{1,0:T(8,128)(2,1)S(1)} fusion(f32[1024,512]{1,0:T(8,128)S(1)} %fusion.3, bf16[1024,1024]{1,0:T(8,128)(2,1)S(1)} %copy-done, bf16[512,1024]{1,0:T(8,128)(2,1)} %collective-permute-done.1, f32[1024]{0:T(1024)S(1)} %bitcast.70, f32[1024]{0:T(1024)S(1)} %get-tuple-element.3, f32[1024]{0:T(1024)S(1)} %get-tuple-element.2), kind=kOutput, calls=%fused_computation.5 | convolution fusion | flops 1080033280 | bytes 6303744 | tf_op jit(solution)/shard_map/dot_general | solution.py:29
  58.7 3.7 %multiply_convert_fusion.2 = bf16[1024,512]{1,0:T(8,128)(2,1)S(1)} fusion(f32[1024,512]{1,0:T(8,128)S(1)} %fusion.6, bf16[1024,1024]{1,0:T(8,128)(2,1)S(1)} %copy-done, bf16[512,1024]{1,0:T(8,128)(2,1)} %collective-permute-done.7, f32[1024]{0:T(1024)S(1)} %bitcast.69, f32[1024]{0:T(1024)S(1)} %get-tuple-element.3, f32[1024]{0:T(1024)S(1)} %get-tuple-element.2), kind=kOutput, calls=%fused_computation.2 | convolution fusion | flops 1080033280 | bytes 6303744 | tf_op jit(solution)/shard_map/dot_general | solution.py:29
  62.4 0.5 fusion.12
  62.9 0.5 fusion.14
  63.4 0.4 fusion.7
  63.8 0.4 convolution_add_fusion.4
  64.3 13.0 %collective-permute-done.9 = bf16[512,1024]{1,0:T(8,128)(2,1)S(1)} collective-permute-done((bf16[512,1024]{1,0:T(8,128)(2,1)}, bf16[512,1024]{1,0:T(8,128)(2,1)S(1)}, u32[]{:S(2)}, u32[]{:S(2)}) %collective-permute-start.9) | collective-permute-done | bytes 1048608 | tf_op jit(solution)/shard_map/ppermute | solution.py:16
  77.2 3.9 %collective-permute-start.11 = (bf16[512,1024]{1,0:T(8,128)(2,1)S(1)}, bf16[512,1024]{1,0:T(8,128)(2,1)S(1)}, u32[]{:S(2)}, u32[]{:S(2)}) collective-permute-start(bf16[512,1024]{1,0:T(8,128)(2,1)S(1)} %collective-permute-done.9), channel_id=1, source_target_pairs={{254,0},{0,2},{2,4},{4,6},{6,8},{8,10},{10,12},{12,14},{14,16},{16... | collective-permute-start | bytes 3145736 | tf_op jit(solution)/shard_map/ppermute | solution.py:16
  81.1 0.8 collective-permute-done.3
  82.0 2.5 %multiply_convert_fusion.4 = bf16[1024,512]{1,0:T(8,128)(2,1)S(1)} fusion(f32[1024,512]{1,0:T(8,128)S(1)} %fusion.4, bf16[1024,1024]{1,0:T(8,128)(2,1)S(1)} %copy-done, bf16[512,1024]{1,0:T(8,128)(2,1)S(1)} %collective-permute-done.3, f32[1024]{0:T(1024)S(1)} %bitcast.68, f32[1024]{0:T(1024)S(1)} %get-tuple-element.3, f32[1024]{0:T(1024)S(1)} %get-tuple-element.2), kind=kOutput, calls=%fused_computation.4 | convolution fusion | flops 1080033280 | bytes 6303744 | tf_op jit(solution)/shard_map/dot_general | solution.py:29
  84.5 2.5 %multiply_convert_fusion.1 = bf16[1024,512]{1,0:T(8,128)(2,1)S(1)} fusion(f32[1024,512]{1,0:T(8,128)S(1)} %fusion.8, bf16[1024,1024]{1,0:T(8,128)(2,1)S(1)} %copy-done, bf16[512,1024]{1,0:T(8,128)(2,1)S(1)} %collective-permute-done.9, f32[1024]{0:T(1024)S(1)} %bitcast.67, f32[1024]{0:T(1024)S(1)} %get-tuple-element.3, f32[1024]{0:T(1024)S(1)} %get-tuple-element.2), kind=kOutput, calls=%fused_computation.1 | convolution fusion | flops 1080033280 | bytes 6303744 | tf_op jit(solution)/shard_map/dot_general | solution.py:29
  87.0 18.3 %collective-permute-done.5 = bf16[512,1024]{1,0:T(8,128)(2,1)S(1)} collective-permute-done((bf16[512,1024]{1,0:T(8,128)(2,1)S(1)}, bf16[512,1024]{1,0:T(8,128)(2,1)S(1)}, u32[]{:S(2)}, u32[]{:S(2)}) %collective-permute-start.5) | collective-permute-done | bytes 1048608 | tf_op jit(solution)/shard_map/ppermute | solution.py:16
  105.3 2.4 %multiply_convert_fusion.3 = bf16[1024,512]{1,0:T(8,128)(2,1)S(1)} fusion(f32[1024,512]{1,0:T(8,128)S(1)} %fusion.5, bf16[1024,1024]{1,0:T(8,128)(2,1)S(1)} %copy-done, bf16[512,1024]{1,0:T(8,128)(2,1)S(1)} %collective-permute-done.5, f32[1024]{0:T(1024)S(1)} %bitcast.66, f32[1024]{0:T(1024)S(1)} %get-tuple-element.3, f32[1024]{0:T(1024)S(1)} %get-tuple-element.2), kind=kOutput, calls=%fused_computation.3 | convolution fusion | flops 1080033280 | bytes 6303744 | tf_op jit(solution)/shard_map/dot_general | solution.py:29
  107.7 0.5 fusion.11
  108.5 2.5 %multiply_convert_fusion = bf16[1024,512]{1,0:T(8,128)(2,1)S(1)} fusion(f32[1024,512]{1,0:T(8,128)S(1)} %fusion.9, bf16[1024,1024]{1,0:T(8,128)(2,1)S(1)} %copy-done, bf16[512,1024]{1,0:T(8,128)(2,1)S(1)} %collective-permute-done.11, f32[1024]{0:T(1024)S(1)} %bitcast.65, f32[1024]{0:T(1024)S(1)} %get-tuple-element.3, f32[1024]{0:T(1024)S(1)} %get-tuple-element.2), kind=kOutput, calls=%fused_computation | convolution fusion | flops 1080033280 | bytes 6303744 | tf_op jit(solution)/shard_map/dot_general | solution.py:29
  111.0 0.5 fusion.13
  111.5 0.5 collective-permute-start.15
  112.0 0.5 convolution_add_fusion.6
  112.5 3.9 %collective-permute-start.13 = (f32[512,128]{1,0:T(8,128)S(1)}, f32[512,128]{1,0:T(8,128)S(1)}, u32[]{:S(2)}, u32[]{:S(2)}) collective-permute-start(f32[512,128]{1,0:T(8,128)S(1)} %convolution_add_fusion.6), channel_id=1, source_target_pairs={{254,0},{0,2},{2,4},{4,6},{6,8},{8,10},{10,12},{12,14},{14,16},{16... | collective-permute-start | bytes 786440 | tf_op jit(solution)/shard_map/ppermute | solution.py:16
  116.4 2.5 %collective-permute-done.15 = f32[512,128]{1,0:T(8,128)S(1)} collective-permute-done((f32[512,128]{1,0:T(8,128)S(1)}, f32[512,128]{1,0:T(8,128)S(1)}, u32[]{:S(2)}, u32[]{:S(2)}) %collective-permute-start.15) | collective-permute-done | bytes 262176 | tf_op jit(solution)/shard_map/ppermute | solution.py:16
  118.9 0.5 convolution_add_fusion.5
  119.5 0.4 convolution_add_fusion.3
  119.9 3.9 %collective-permute-start.14 = (f32[512,128]{1,0:T(8,128)S(1)}, f32[512,128]{1,0:T(8,128)S(1)}, u32[]{:S(2)}, u32[]{:S(2)}) collective-permute-start(f32[512,128]{1,0:T(8,128)S(1)} %add.45), channel_id=1, source_target_pairs={{254,0},{0,2},{2,4},{4,6},{6,8},{8,10},{10,12},{12,14},{14,16},{16... | collective-permute-start | bytes 786440 | tf_op jit(solution)/shard_map/ppermute | solution.py:16
  123.8 2.9 %collective-permute-done.16 = f32[512,128]{1,0:T(8,128)S(1)} collective-permute-done((f32[512,128]{1,0:T(8,128)S(1)}, f32[512,128]{1,0:T(8,128)S(1)}, u32[]{:S(2)}, u32[]{:S(2)}) %collective-permute-start.16) | collective-permute-done | bytes 262176 | tf_op jit(solution)/shard_map/ppermute | solution.py:16
  126.8 1.5 collective-permute-start.17
  128.2 1.2 fusion
  129.5 7.5 %collective-permute-done.17 = f32[512,128]{1,0:T(8,128)S(1)} collective-permute-done((f32[512,128]{1,0:T(8,128)S(1)}, f32[512,128]{1,0:T(8,128)S(1)}, u32[]{:S(2)}, u32[]{:S(2)}) %collective-permute-start.17) | collective-permute-done | bytes 262176 | tf_op jit(solution)/shard_map/ppermute | solution.py:16
  137.0 0.7 add_add_fusion
  137.7 1.6 convolution_add_fusion.1
  139.3 1.2 convolution_add_fusion
  140.6 19.7 %reduce-scatter.2.cloned.1.call-done = f32[256,128]{1,0:T(8,128)} async-done(((f32[512,128]{1,0:T(8,128)}), f32[256,128]{1,0:T(8,128)}) %reduce-scatter.2.cloned.1.call-update) | async-done | bytes 131088 | tf_op jit(solution)/shard_map/reduce_scatter | solution.py:126
  (47 shorter events, 2.3 us)
Async XLA Ops:
  7.2 12.8 %copy-start = (bf16[1024,1024]{1,0:T(8,128)(2,1)S(1)}, bf16[1024,1024]{1,0:T(8,128)(2,1)}, u32[]{:S(2)}) copy-start(bf16[1024,1024]{1,0:T(8,128)(2,1)} %param.8) | copy-start | bytes 6291460
  7.2 153.1 %reduce-scatter.2.cloned.1.call-start = ((), (), s32[]{:S(2)}) async-start(), calls=%async_computation.1 | async-start | bytes 393216 | tf_op jit(solution)/shard_map/reduce_scatter | solution.py:126
  7.2 25.9 %collective-permute-start.6 = (bf16[512,128]{1,0:T(8,128)(2,1)}, bf16[512,128]{1,0:T(8,128)(2,1)S(1)}, u32[]{:S(2)}, u32[]{:S(2)}) collective-permute-start(bf16[512,128]{1,0:T(8,128)(2,1)} %param.11), channel_id=1, source_target_pairs={{254,0},{0,2},{2,4},{4,6},{6,8},{8,10},{10,12},{12,14},{14,16},{16... | collective-permute-start | bytes 393224 | tf_op jit(solution)/shard_map/ppermute | solution.py:16
  11.6 13.5 %collective-permute-start = (bf16[512,128]{1,0:T(8,128)(2,1)}, bf16[512,128]{1,0:T(8,128)(2,1)S(1)}, u32[]{:S(2)}, u32[]{:S(2)}) collective-permute-start(bf16[512,128]{1,0:T(8,128)(2,1)} %param.11), channel_id=1, source_target_pairs={{2,0},{4,2},{6,4},{8,6},{10,8},{12,10},{14,12},{16,14},{18,16},{20... | collective-permute-start | bytes 393224 | tf_op jit(solution)/shard_map/ppermute | solution.py:16
  11.6 42.8 %collective-permute-start.7 = (bf16[512,1024]{1,0:T(8,128)(2,1)}, bf16[512,1024]{1,0:T(8,128)(2,1)}, u32[]{:S(2)}, u32[]{:S(2)}) collective-permute-start(bf16[512,1024]{1,0:T(8,128)(2,1)} %param.9), channel_id=1, source_target_pairs={{254,0},{0,2},{2,4},{4,6},{6,8},{8,10},{10,12},{12,14},{14,16},{16... | collective-permute-start | bytes 3145736 | tf_op jit(solution)/shard_map/ppermute | solution.py:16
  14.9 39.7 %collective-permute-start.1 = (bf16[512,1024]{1,0:T(8,128)(2,1)}, bf16[512,1024]{1,0:T(8,128)(2,1)}, u32[]{:S(2)}, u32[]{:S(2)}) collective-permute-start(bf16[512,1024]{1,0:T(8,128)(2,1)} %param.9), channel_id=1, source_target_pairs={{2,0},{4,2},{6,4},{8,6},{10,8},{12,10},{14,12},{16,14},{18,16},{20... | collective-permute-start | bytes 3145736 | tf_op jit(solution)/shard_map/ppermute | solution.py:16
  19.9 2.6 %copy-start.7 = (f32[4,1024]{1,0:T(4,128)S(1)}, f32[4,1024]{1,0:T(4,128)}, u32[]{:S(2)}) copy-start(f32[4,1024]{1,0:T(4,128)} %param.15) | copy-start | bytes 49156
  19.9 2.6 %copy-start.8 = (f32[4,1024]{1,0:T(4,128)S(1)}, f32[4,1024]{1,0:T(4,128)}, u32[]{:S(2)}) copy-start(f32[4,1024]{1,0:T(4,128)} %param.14) | copy-start | bytes 49156
  19.9 2.6 %copy-start.9 = (s32[1024]{0:T(1024)S(1)}, s32[1024]{0:T(1024)}, u32[]{:S(2)}) copy-start(s32[1024]{0:T(1024)} %param.13) | copy-start | bytes 12292
  20.0 2.7 %copy-start.1 = (bf16[1024,128]{1,0:T(8,128)(2,1)S(1)}, bf16[1024,128]{1,0:T(8,128)(2,1)}, u32[]{:S(2)}) copy-start(bf16[1024,128]{1,0:T(8,128)(2,1)} %param.10) | copy-start | bytes 786436
  20.0 2.7 %copy-start.6 = (bf16[512,128]{1,0:T(8,128)(2,1)S(1)}, bf16[512,128]{1,0:T(8,128)(2,1)}, u32[]{:S(2)}) copy-start(bf16[512,128]{1,0:T(8,128)(2,1)} %param.11) | copy-start | bytes 393220
  25.2 21.1 %collective-permute-start.2 = (bf16[512,128]{1,0:T(8,128)(2,1)S(1)}, bf16[512,128]{1,0:T(8,128)(2,1)S(1)}, u32[]{:S(2)}, u32[]{:S(2)}) collective-permute-start(bf16[512,128]{1,0:T(8,128)(2,1)S(1)} %collective-permute-done), channel_id=1, source_target_pairs={{2,0},{4,2},{6,4},{8,6},{10,8},{12,10},{14,12},{16,14},{18,16},{20... | collective-permute-start | bytes 393224 | tf_op jit(solution)/shard_map/ppermute | solution.py:16
  33.1 8.3 %collective-permute-start.8 = (bf16[512,128]{1,0:T(8,128)(2,1)S(1)}, bf16[512,128]{1,0:T(8,128)(2,1)S(1)}, u32[]{:S(2)}, u32[]{:S(2)}) collective-permute-start(bf16[512,128]{1,0:T(8,128)(2,1)S(1)} %collective-permute-done.6), channel_id=1, source_target_pairs={{254,0},{0,2},{2,4},{4,6},{6,8},{8,10},{10,12},{12,14},{14,16},{16... | collective-permute-start | bytes 393224 | tf_op jit(solution)/shard_map/ppermute | solution.py:16
  41.5 12.5 %collective-permute-start.10 = (bf16[512,128]{1,0:T(8,128)(2,1)S(1)}, bf16[512,128]{1,0:T(8,128)(2,1)S(1)}, u32[]{:S(2)}, u32[]{:S(2)}) collective-permute-start(bf16[512,128]{1,0:T(8,128)(2,1)S(1)} %collective-permute-done.8), channel_id=1, source_target_pairs={{254,0},{0,2},{2,4},{4,6},{6,8},{8,10},{10,12},{12,14},{14,16},{16... | collective-permute-start | bytes 393224 | tf_op jit(solution)/shard_map/ppermute | solution.py:16
  46.2 7.3 %collective-permute-start.4 = (bf16[512,128]{1,0:T(8,128)(2,1)S(1)}, bf16[512,128]{1,0:T(8,128)(2,1)S(1)}, u32[]{:S(2)}, u32[]{:S(2)}) collective-permute-start(bf16[512,128]{1,0:T(8,128)(2,1)S(1)} %collective-permute-done.2), channel_id=1, source_target_pairs={{2,0},{4,2},{6,4},{8,6},{10,8},{12,10},{14,12},{16,14},{18,16},{20... | collective-permute-start | bytes 393224 | tf_op jit(solution)/shard_map/ppermute | solution.py:16
  54.0 4.7 %copy-start.4 = (bf16[512,128]{1,0:T(8,128)(2,1)}, bf16[512,128]{1,0:T(8,128)(2,1)S(1)}, u32[]{:S(2)}) copy-start(bf16[512,128]{1,0:T(8,128)(2,1)S(1)} %collective-permute-done.10) | copy-start | bytes 393220
  54.4 22.8 %collective-permute-start.9 = (bf16[512,1024]{1,0:T(8,128)(2,1)}, bf16[512,1024]{1,0:T(8,128)(2,1)S(1)}, u32[]{:S(2)}, u32[]{:S(2)}) collective-permute-start(bf16[512,1024]{1,0:T(8,128)(2,1)} %collective-permute-done.7), channel_id=1, source_target_pairs={{254,0},{0,2},{2,4},{4,6},{6,8},{8,10},{10,12},{12,14},{14,16},{16... | collective-permute-start | bytes 3145736 | tf_op jit(solution)/shard_map/ppermute | solution.py:16
  54.5 27.4 %collective-permute-start.3 = (bf16[512,1024]{1,0:T(8,128)(2,1)}, bf16[512,1024]{1,0:T(8,128)(2,1)S(1)}, u32[]{:S(2)}, u32[]{:S(2)}) collective-permute-start(bf16[512,1024]{1,0:T(8,128)(2,1)} %collective-permute-done.1), channel_id=1, source_target_pairs={{2,0},{4,2},{6,4},{8,6},{10,8},{12,10},{14,12},{16,14},{18,16},{20... | collective-permute-start | bytes 3145736 | tf_op jit(solution)/shard_map/ppermute | solution.py:16
  77.2 31.3 %collective-permute-start.11 = (bf16[512,1024]{1,0:T(8,128)(2,1)S(1)}, bf16[512,1024]{1,0:T(8,128)(2,1)S(1)}, u32[]{:S(2)}, u32[]{:S(2)}) collective-permute-start(bf16[512,1024]{1,0:T(8,128)(2,1)S(1)} %collective-permute-done.9), channel_id=1, source_target_pairs={{254,0},{0,2},{2,4},{4,6},{6,8},{8,10},{10,12},{12,14},{14,16},{16... | collective-permute-start | bytes 3145736 | tf_op jit(solution)/shard_map/ppermute | solution.py:16
  82.0 23.3 %collective-permute-start.5 = (bf16[512,1024]{1,0:T(8,128)(2,1)S(1)}, bf16[512,1024]{1,0:T(8,128)(2,1)S(1)}, u32[]{:S(2)}, u32[]{:S(2)}) collective-permute-start(bf16[512,1024]{1,0:T(8,128)(2,1)S(1)} %collective-permute-done.3), channel_id=1, source_target_pairs={{2,0},{4,2},{6,4},{8,6},{10,8},{12,10},{14,12},{16,14},{18,16},{20... | collective-permute-start | bytes 3145736 | tf_op jit(solution)/shard_map/ppermute | solution.py:16
  108.2 3.8 %collective-permute-start.12 = (f32[512,128]{1,0:T(8,128)S(1)}, f32[512,128]{1,0:T(8,128)S(1)}, u32[]{:S(2)}, u32[]{:S(2)}) collective-permute-start(f32[512,128]{1,0:T(8,128)S(1)} %fusion.11), channel_id=1, source_target_pairs={{254,0},{0,2},{2,4},{4,6},{6,8},{8,10},{10,12},{12,14},{14,16},{16... | collective-permute-start | bytes 786440 | tf_op jit(solution)/shard_map/ppermute | solution.py:16
  111.0 8.3 %copy-start.2 = (bf16[1024,512]{1,0:T(8,128)(2,1)}, bf16[1024,512]{1,0:T(8,128)(2,1)S(1)}, u32[]{:S(2)}) copy-start(bf16[1024,512]{1,0:T(8,128)(2,1)S(1)} %multiply_convert_fusion) | copy-start | bytes 3145732
  111.5 7.4 %collective-permute-start.15 = (f32[512,128]{1,0:T(8,128)S(1)}, f32[512,128]{1,0:T(8,128)S(1)}, u32[]{:S(2)}, u32[]{:S(2)}) collective-permute-start(f32[512,128]{1,0:T(8,128)S(1)} %fusion.13), channel_id=1, source_target_pairs={{2,0},{4,2},{6,4},{8,6},{10,8},{12,10},{14,12},{16,14},{18,16},{20... | collective-permute-start | bytes 786440 | tf_op jit(solution)/shard_map/ppermute | solution.py:16
  112.5 7.4 %collective-permute-start.13 = (f32[512,128]{1,0:T(8,128)S(1)}, f32[512,128]{1,0:T(8,128)S(1)}, u32[]{:S(2)}, u32[]{:S(2)}) collective-permute-start(f32[512,128]{1,0:T(8,128)S(1)} %convolution_add_fusion.6), channel_id=1, source_target_pairs={{254,0},{0,2},{2,4},{4,6},{6,8},{8,10},{10,12},{12,14},{14,16},{16... | collective-permute-start | bytes 786440 | tf_op jit(solution)/shard_map/ppermute | solution.py:16
  119.4 7.4 %collective-permute-start.16 = (f32[512,128]{1,0:T(8,128)S(1)}, f32[512,128]{1,0:T(8,128)S(1)}, u32[]{:S(2)}, u32[]{:S(2)}) collective-permute-start(f32[512,128]{1,0:T(8,128)S(1)} %convolution_add_fusion.5), channel_id=1, source_target_pairs={{2,0},{4,2},{6,4},{8,6},{10,8},{12,10},{14,12},{16,14},{18,16},{20... | collective-permute-start | bytes 786440 | tf_op jit(solution)/shard_map/ppermute | solution.py:16
  119.9 9.5 %collective-permute-start.14 = (f32[512,128]{1,0:T(8,128)S(1)}, f32[512,128]{1,0:T(8,128)S(1)}, u32[]{:S(2)}, u32[]{:S(2)}) collective-permute-start(f32[512,128]{1,0:T(8,128)S(1)} %add.45), channel_id=1, source_target_pairs={{254,0},{0,2},{2,4},{4,6},{6,8},{8,10},{10,12},{12,14},{14,16},{16... | collective-permute-start | bytes 786440 | tf_op jit(solution)/shard_map/ppermute | solution.py:16
  126.8 10.2 %collective-permute-start.17 = (f32[512,128]{1,0:T(8,128)S(1)}, f32[512,128]{1,0:T(8,128)S(1)}, u32[]{:S(2)}, u32[]{:S(2)}) collective-permute-start(f32[512,128]{1,0:T(8,128)S(1)} %add.48), channel_id=1, source_target_pairs={{2,0},{4,2},{6,4},{8,6},{10,8},{12,10},{14,12},{16,14},{18,16},{20... | collective-permute-start | bytes 786440 | tf_op jit(solution)/shard_map/ppermute | solution.py:16
  129.5 9.9 %copy-start.5 = (bf16[512,128]{1,0:T(8,128)(2,1)S(1)}, bf16[512,128]{1,0:T(8,128)(2,1)}, u32[]{:S(2)}) copy-start(bf16[512,128]{1,0:T(8,128)(2,1)} %copy-done.4) | copy-start | bytes 393220
  137.7 1.6 copy-start.3
Sparse Core Ops, SparseCore 0:
  137.9 22.3 reduce-scatter.1
where the time goes:
time: 167 us
  waiting for transfers between devices  79.9 us (48%)
  starting transfers between devices  38 us (23%)
  matrix products  33.1 us (20%)
  between operations  14.4 us (9%)
    ppermute x18, waiting for transfers between devices, from_behind(): return lax.ppermute(block, axis, route)  60.1 us
    ppermute x18, starting transfers between devices, from_behind(): return lax.ppermute(block, axis, route)  38 us
    dot_general x14, matrix products, contract_rows(): lax.dot_general(left, right, (((1,), (1,)), ((), ())), preferred_element_...  24 us
    reduce_scatter x1, waiting for transfers between devices, shards(): lax.psum_scatter(item_total, 'rep', scatter_dimension=0, tiled=True)  19.7 us
    dot_general x6, matrix products, shards(): jnp.dot(grad_pair, current[1], preferred_element_type=jnp.float32)  5.33 us
  transfers between devices with their start and end apart: 19, of which 10 were waited for; matrix products, arithmetic and copies ran while one was open for 20% of the time, Pallas kernels for 0%

commit v1 on v0

v1 whole, which is shorter than its diff:
```python
import functools
import math

import jax
import jax.numpy as jnp
from jax import lax
from jax.experimental import pallas as pl
from jax.experimental.pallas import tpu as pltpu
from jax.sharding import PartitionSpec as P

logit_cap = 10.0
score_gain = 3.0
loss_weight = 8.0
log2e = 1.0 / math.log(2.0)
never = 1e9
AXES = ("items", "rep")


def edges(n_items, move):
    pairs = []
    for flat in range(n_items * 2):
        item, rep = flat // 2, flat % 2
        pos, y, core = item // 4, (item // 2 % 2) * 2 + rep, item % 2
        pos, y, core = move(pos, y, core)
        pos = pos % (n_items // 4)
        target = ((pos * 2 + y // 2) * 2 + core) * 2 + y % 2
        pairs.append((flat, target))
    return pairs


def step(y):
    return -1 if y < 2 else 1


def far(p, y, c):
    return (p + 1, y, 0) if c == 1 else (p - 1, y, 1)


def relay_one(p, y, c):
    if y < 2:
        return (p + 1, y, 0) if c == 0 else (p, 3 - y, 0)
    return (p - 1, y, 1) if c == 1 else (p, 3 - y, 1)


def relay_two(p, y, c):
    if y < 2:
        return (p + 1, y, 0) if c == 0 else (p, y ^ 1, 1)
    return (p - 1, y, 1) if c == 1 else (p, y ^ 1, 0)


def cross(p, y, c):
    return p, 3 - y, c


def pair(p, y, c):
    return p, y ^ 1, c


def two(p, y, c):
    return p, y ^ 2, c


def core(p, y, c):
    return p, y, 1 - c


def diag(p, y, c):
    return p + step(y), 3 - y, c


def diag_two(p, y, c):
    return p + step(y), y ^ 2, c


def diag_two_core(p, y, c):
    return p + step(y), y ^ 2, 1 - c


def visit_kernel(row, first, scales, zt_ref, zs_ref, tq_ref, sqt_ref, sq_ref, piece_ref, *refs):
    q_ref, term_ref = refs[-2:]
    width = tq_ref.shape[0]
    teacher = piece_ref[:, :width]
    student = piece_ref[:, width:]
    t_raw = jnp.dot(teacher, tq_ref[...], preferred_element_type=jnp.float32)
    s_raw = jnp.dot(student, sqt_ref[...], preferred_element_type=jnp.float32)
    t_tanh = jnp.tanh(t_raw * scales[0])
    s_tanh = jnp.tanh(s_raw * scales[1])
    t_exp = jnp.exp2(t_tanh * (logit_cap * log2e) - zt_ref[row : row + 1, :])
    s_exp = jnp.exp2(s_tanh * (logit_cap * log2e) - zs_ref[row : row + 1, :])
    grads = ((s_exp - t_exp) * (1.0 - s_tanh * s_tanh)).astype(jnp.bfloat16)
    term_ref[...] = jnp.dot(grads, sq_ref[...], preferred_element_type=jnp.float32)
    q_part = lax.dot_general(
        student, grads, (((0,), (0,)), ((), ())), preferred_element_type=jnp.float32
    )
    q_ref[...] = q_part if first else refs[0][...] + q_part


def visit(row, shared, scales, piece, q):
    rows, width = piece.shape[0], shared[4].shape[1]
    requests = shared[4].shape[0]
    vmem = pl.BlockSpec(memory_space=pltpu.VMEM)
    operands = (*shared, piece) if q is None else (*shared, piece, q)
    return pl.pallas_call(
        functools.partial(visit_kernel, row, q is None, scales),
        out_shape=(
            jax.ShapeDtypeStruct((width, requests), jnp.float32),
            jax.ShapeDtypeStruct((rows, width), jnp.float32),
        ),
        in_specs=[vmem] * len(operands),
        out_specs=(vmem, vmem),
        compiler_params=pltpu.CompilerParams(vmem_limit_bytes=24 << 20),
    )(*operands)


def shards(
    teacher_queries,
    teacher_items,
    student_queries,
    student_items,
    block_mask,
    pass_index,
    teacher_norms,
    student_norms,
):
    n_items = lax.axis_size("items")
    rows = teacher_queries.shape[0]
    blocks = block_mask.shape[0]
    span = teacher_items.shape[0]
    half = span // 2
    quarter = half // 2
    teacher_scale = score_gain / math.sqrt(teacher_queries.shape[1])
    student_scale = score_gain / math.sqrt(student_queries.shape[1])
    scales = (teacher_scale / logit_cap, student_scale / logit_cap)

    item = lax.axis_index("items")
    rep = lax.axis_index("rep")
    core_id = item % 2
    type_b = item // 2 % 2

    def send(block, move):
        return lax.ppermute(block, AXES, edges(n_items, move))

    mine = rep * half
    own_half = jnp.concatenate(
        [
            lax.dynamic_slice_in_dim(teacher_items, mine, half, 0),
            lax.dynamic_slice_in_dim(student_items, mine, half, 0),
        ],
        axis=1,
    )
    cross_a = send(own_half[:quarter], cross)
    cross_b = send(own_half[quarter:], cross)
    own = jnp.concatenate([teacher_items, student_items], axis=1)
    far_span = send(own, far)
    core_span = send(own, core)

    passes = jnp.arange(teacher_norms.shape[0], dtype=jnp.int32)
    picked = (pass_index[None, :] == passes[:, None]).astype(jnp.float32)
    fold = math.log2(loss_weight * student_scale)
    zt = jnp.sum(teacher_norms * picked, axis=0) * log2e - fold
    zs = jnp.sum(student_norms * picked, axis=0) * log2e - fold
    near = 1 - 2 * core_id
    ahead = 2 - 4 * type_b
    offsets = jnp.stack([0 * near, near, -3 * near, ahead, ahead + near, -ahead, near - ahead])
    reach = block_mask.shape[1] // 2
    chosen = offsets[:, None, None] + reach == jnp.arange(2 * reach + 1)[None, None, :]
    on = jnp.any(chosen & (block_mask[None] != 0), axis=2)
    on = jnp.broadcast_to(on[:, :, None], (on.shape[0], blocks, rows // blocks))
    on = on.reshape(on.shape[0], rows)
    shared = (
        jnp.where(on, zt[None], never),
        jnp.where(on, zs[None], never),
        teacher_queries.T,
        student_queries.T,
        student_queries,
    )

    q, own_term = visit(0, shared, scales, own, None)
    q, core_term = visit(1, shared, scales, core_span, q)

    pair_a = send(cross_a, pair)
    pair_b = send(cross_b, pair)
    cross_half = jnp.concatenate([cross_a, cross_b])
    pair_half = jnp.concatenate([pair_a, pair_b])
    relays = jnp.logical_xor(type_b == 0, core_id == 1)
    far_half = lax.dynamic_slice_in_dim(far_span, mine, half, 0)
    next_one = send(jnp.where(relays, cross_half, far_half), relay_one)
    next_two = send(jnp.where(relays, pair_half, next_one), relay_two)

    q, far_term = visit(2, shared, scales, far_span, q)
    far_back = send(far_term, far)
    across = jnp.concatenate([cross_half, pair_half])
    across_core = send(across, core)
    q, across_term = visit(3, shared, scales, across, q)
    q, across_core_term = visit(4, shared, scales, across_core, q)
    next_one_core = send(next_one, core)
    q, one_term = visit(5, shared, scales, next_one, q)
    q, one_core_term = visit(6, shared, scales, next_one_core, q)
    swapped = send(jnp.concatenate([core_term, across_core_term, one_core_term]), core)
    own_total = own_term + far_back + swapped[:span]
    across_total = across_term + swapped[span : 2 * span]
    one_total = one_term + swapped[2 * span :]
    pair_back = send(lax.dynamic_slice_in_dim(own_total, half - mine, half, 0), pair)
    cross_back = send(across_total[:half], cross)
    two_back = send(across_total[half:], two)
    one_back = send(one_total, diag)
    total = lax.dynamic_slice_in_dim(own_total, mine, half, 0)
    total = total + pair_back + cross_back + two_back + one_back

    next_two_core = send(next_two, core)
    q, two_term = visit(5, shared, scales, next_two, q)
    last_back = send(two_term, diag_two)
    q, two_core_term = visit(6, shared, scales, next_two_core, q)
    last_core_back = send(two_core_term, diag_two_core)
    return q.T, total + last_back + last_core_back


def solution(mesh):
    return jax.shard_map(
        shards,
        mesh=mesh,
        in_specs=(
            P(("items", "rep"), None),
            P("items", None),
            P(("items", "rep"), None),
            P("items", None),
            P(("items", "rep"), None),
            P(("items", "rep")),
            P(None, ("items", "rep")),
            P(None, ("items", "rep")),
        ),
        out_specs=(P(("items", "rep"), None), P(("items", "rep"), None)),
        check_vma=False,
    )
```

time: 167 us -> 105 us (0.63)
  waiting for transfers between devices: 79.9 us -> 24 us
  matrix products: 33.1 us -> 0 us
  Pallas kernels: 0 us -> 25 us
  between operations: 14.4 us -> 0.95 us
  local copies, waits for them, and re-layouts: 0.22 us -> 13.5 us
  other arithmetic: 1.56 us -> 6.09 us
  starting transfers between devices: 38 us -> 34.8 us
    ppermute x18 -> x19, waiting for transfers between devices: 60.1 us -> 24 us  [send(): return lax.ppermute(block, AXES, edges(n_items, move))]
    dot_general x28 -> x0, matrix products: 33.1 us -> none  [the longest x14 24 us: contract_rows(): lax.dot_general(left, right, (((1,), (1,)), ((), ())), preferred_element_...]
    pallas_call x0 -> x9, Pallas kernels: none -> 25 us  [visit(): pl.pallas_call(functools.partial(visit_kernel, row, q is None, scales), o...]
    reduce_scatter x1 -> x0, waiting for transfers between devices: 19.7 us -> none  [shards(): lax.psum_scatter(item_total, 'rep', scatter_dimension=0, tiled=True)]
    unnamed x20 -> x41, local copies, waits for them, and re-layouts: 0.06 us -> 11.7 us
    ppermute x18 -> x19, starting transfers between devices: 38 us -> 34.8 us  [send(): return lax.ppermute(block, AXES, edges(n_items, move))]
    add x3 -> x4, other arithmetic: 0.81 us -> 3.74 us  [the longest x1 1.6 us: shards(): return (q.T, total + last_back + last_core_back)]
  transfers between devices with their start and end apart: 19 -> 19, of which waited for: 10 -> 6; matrix products, arithmetic and copies ran while one was open for 20% -> 13% of each run, Pallas kernels for 0% -> 24%
where the time goes in v1:
time: 105 us; the launch traced here: 104 us
  starting transfers between devices  34.8 us (33%)
  Pallas kernels  25 us (24%)
  waiting for transfers between devices  24 us (23%)
  local copies, waits for them, and re-layouts  13.5 us (13%)
  other arithmetic  6.09 us (6%)
    ppermute x19, starting transfers between devices, send(): return lax.ppermute(block, AXES, edges(n_items, move))  34.8 us
    pallas_call x9, Pallas kernels, visit(): pl.pallas_call(functools.partial(visit_kernel, row, q is None, scales), o...  25 us
    ppermute x19, waiting for transfers between devices, send(): return lax.ppermute(block, AXES, edges(n_items, move))  24 us
    unnamed x41, local copies, waits for them, and re-layouts  11.7 us
  transfers between devices with their start and end apart: 19, of which 6 were waited for; matrix products, arithmetic and copies ran while one was open for 13% of the time, Pallas kernels for 24%

profile of v1, /device:TPU:1, one launch (start us, length us, event | category | flops | bytes accessed | tf_op | source)
XLA Modules:
  0.0 104.4 jit_solution(7060858862715814378)
XLA Ops:
  0.6 2.4 %constant_dynamic-update-slice_fusion.1 = bf16[512,1152]{1,0:T(8,128)(2,1)} fusion(bf16[512,1024]{1,0:T(8,128)(2,1)} %param.9), kind=kLoop, calls=%fused_computation.18 | loop fusion | bytes 2097152
  3.0 0.7 constant_dynamic-update-slice_fusion.piece_ref
  3.7 3.2 %collective-permute-start.10 = (bf16[512,1152]{1,0:T(8,128)(2,1)}, bf16[512,1152]{1,0:T(8,128)(2,1)}, u32[]{:S(2)}, u32[]{:S(2)}) collective-permute-start(bf16[512,1152]{1,0:T(8,128)(2,1)} %constant_dynamic-update-slice_fusion.piece_ref), channel_id=1, source_target_pairs={{0,2},{1,3},{2,0},{3,1},{4,6},{5,7},{6,4},{7,5},{8,10},{9,11},{10,... | collective-permute-start | bytes 3538952 | tf_op jit(solution)/shard_map/ppermute | solution.py:141
  7.1 2.2 %collective-permute-start = (bf16[128,1152]{1,0:T(8,128)(2,1)S(1)}, bf16[128,1152]{1,0:T(8,128)(2,1)S(1)}, u32[]{:S(2)}, u32[]{:S(2)}) collective-permute-start(bf16[128,1152]{1,0:T(8,128)(2,1)S(1)} %get-tuple-element.46), channel_id=1, source_target_pairs={{0,5},{1,4},{2,7},{3,6},{4,1},{5,0},{6,3},{7,2},{8,13},{9,12},{10,... | collective-permute-start | bytes 884744 | tf_op jit(solution)/shard_map/ppermute | solution.py:141
  9.3 0.6 collective-permute-start.2
  10.0 3.9 %collective-permute-done = bf16[128,1152]{1,0:T(8,128)(2,1)S(1)} collective-permute-done((bf16[128,1152]{1,0:T(8,128)(2,1)S(1)}, bf16[128,1152]{1,0:T(8,128)(2,1)S(1)}, u32[]{:S(2)}, u32[]{:S(2)}) %collective-permute-start) | collective-permute-done | bytes 294944 | tf_op jit(solution)/shard_map/ppermute | solution.py:141
  14.0 3.5 %collective-permute-done.2 = bf16[128,1152]{1,0:T(8,128)(2,1)S(1)} collective-permute-done((bf16[128,1152]{1,0:T(8,128)(2,1)S(1)}, bf16[128,1152]{1,0:T(8,128)(2,1)S(1)}, u32[]{:S(2)}, u32[]{:S(2)}) %collective-permute-start.2) | collective-permute-done | bytes 294944 | tf_op jit(solution)/shard_map/ppermute | solution.py:141
  17.4 0.8 constant_dynamic-update-slice_fusion.5
  18.2 0.7 constant_dynamic-update-slice_fusion.4
  18.9 4.2 %collective-permute-done.4.piece_ref = bf16[512,1152]{1,0:T(8,128)(2,1)S(1)} collective-permute-done((bf16[512,1152]{1,0:T(8,128)(2,1)}, bf16[512,1152]{1,0:T(8,128)(2,1)S(1)}, u32[]{:S(2)}, u32[]{:S(2)}) %collective-permute-start.4) | collective-permute-done | bytes 1179680 | tf_op jit(solution)/shard_map/ppermute | solution.py:141
  23.1 0.1 maximum_select_fusion.1
  23.3 7.1 %collective-permute-start.5 = (bf16[256,1152]{1,0:T(8,128)(2,1)S(1)}, bf16[256,1152]{1,0:T(8,128)(2,1)S(1)}, u32[]{:S(2)}, u32[]{:S(2)}) collective-permute-start(bf16[256,1152]{1,0:T(8,128)(2,1)S(1)} %maximum_select_fusion.1), channel_id=1, source_target_pairs={{0,8},{1,9},{2,5},{3,4},{4,3},{5,2},{6,254},{7,255},{8,16},{9,17},... | collective-permute-start | bytes 1769480 | tf_op jit(solution)/shard_map/ppermute | solution.py:141
  30.3 0.8 constant_dynamic-update-slice_fusion.3
  31.1 0.7 constant_dynamic-update-slice_fusion.2.piece_ref
  31.9 0.3 collective-permute-start.9
  32.2 6.0 %collective-permute-done.5.piece_ref = bf16[256,1152]{1,0:T(8,128)(2,1)S(1)} collective-permute-done((bf16[256,1152]{1,0:T(8,128)(2,1)S(1)}, bf16[256,1152]{1,0:T(8,128)(2,1)S(1)}, u32[]{:S(2)}, u32[]{:S(2)}) %collective-permute-start.5) | collective-permute-done | bytes 589856 | tf_op jit(solution)/shard_map/ppermute | solution.py:141
  38.2 2.7 %collective-permute-start.8 = (bf16[256,1152]{1,0:T(8,128)(2,1)S(1)}, bf16[256,1152]{1,0:T(8,128)(2,1)}, u32[]{:S(2)}, u32[]{:S(2)}) collective-permute-start(bf16[256,1152]{1,0:T(8,128)(2,1)S(1)} %collective-permute-done.5.piece_ref), channel_id=1, source_target_pairs={{0,2},{1,3},{2,0},{3,1},{4,6},{5,7},{6,4},{7,5},{8,10},{9,11},{10,... | collective-permute-start | bytes 1769480 | tf_op jit(solution)/shard_map/ppermute | solution.py:141
  40.9 1.0 maximum_select_fusion
  41.9 1.3 %collective-permute-start.6 = (bf16[256,1152]{1,0:T(8,128)(2,1)}, bf16[256,1152]{1,0:T(8,128)(2,1)}, u32[]{:S(2)}, u32[]{:S(2)}) collective-permute-start(bf16[256,1152]{1,0:T(8,128)(2,1)} %maximum_select_fusion), channel_id=1, source_target_pairs={{0,8},{1,9},{2,3},{3,2},{4,5},{5,4},{6,254},{7,255},{8,16},{9,17},... | collective-permute-start | bytes 1769480 | tf_op jit(solution)/shard_map/ppermute | solution.py:141
  43.2 0.1 and_reduce_fusion
  43.4 0.1 reshape.97
  43.5 3.1 %copy.14 = bf16[1024,1024]{0,1:T(8,128)(2,1)S(1)} copy(bf16[1024,1024]{1,0:T(8,128)(2,1)} %param.8) | data formatting | bytes 4194304 | tf_op args[0]
  46.6 0.1 copy.15
  46.7 3.4 %shard_map.95 = (f32[128,1024]{1,0:T(8,128)S(1)}, f32[512,128]{1,0:T(8,128)S(1)}) custom-call(f32[7,1024]{1,0:T(8,128)S(1)} %get-tuple-element.51.zt_ref, f32[7,1024]{1,0:T(8,128)S(1)} %get-tuple-element.50.zs_ref, bf16[1024,1024]{1,0:T(8,128)(2,1)S(1)} %bitcast.9, bf16[128,1024]{1,0:T(8,128)(2,1)S(1)} %bitcast.18, bf16[1024,128]{1,0:T(8,128)(2,1)S(1)} %copy-done, ...), custom_call_target="tpu_custom_call" | custom-call | tf_op jit(solution)/shard_map/pallas_call | solution.py:103
  50.2 3.5 %shard_map.96 = (f32[128,1024]{1,0:T(8,128)S(1)}, f32[512,128]{1,0:T(8,128)S(1)}) custom-call(f32[7,1024]{1,0:T(8,128)S(1)} %get-tuple-element.51.zt_ref, f32[7,1024]{1,0:T(8,128)S(1)} %get-tuple-element.50.zs_ref, bf16[1024,1024]{1,0:T(8,128)(2,1)S(1)} %bitcast.10, bf16[128,1024]{1,0:T(8,128)(2,1)S(1)} %bitcast.19, bf16[1024,128]{1,0:T(8,128)(2,1)S(1)} %copy-done, ...), custom_call_target="tpu_custom_call" | custom-call | tf_op jit(solution)/shard_map/pallas_call | solution.py:103
  53.7 2.9 %shard_map.97 = (f32[128,1024]{1,0:T(8,128)S(1)}, f32[512,128]{1,0:T(8,128)}) custom-call(f32[7,1024]{1,0:T(8,128)S(1)} %get-tuple-element.51.zt_ref, f32[7,1024]{1,0:T(8,128)S(1)} %get-tuple-element.50.zs_ref, bf16[1024,1024]{1,0:T(8,128)(2,1)S(1)} %bitcast.11, bf16[128,1024]{1,0:T(8,128)(2,1)S(1)} %bitcast.20, bf16[1024,128]{1,0:T(8,128)(2,1)S(1)} %copy-done, ...), custom_call_target="tpu_custom_call" | custom-call | tf_op jit(solution)/shard_map/pallas_call | solution.py:103
  56.6 3.4 %shard_map.98 = (f32[128,1024]{1,0:T(8,128)S(1)}, f32[512,128]{1,0:T(8,128)S(1)}) custom-call(f32[7,1024]{1,0:T(8,128)S(1)} %get-tuple-element.51.zt_ref, f32[7,1024]{1,0:T(8,128)S(1)} %get-tuple-element.50.zs_ref, bf16[1024,1024]{1,0:T(8,128)(2,1)S(1)} %bitcast.12, bf16[128,1024]{1,0:T(8,128)(2,1)S(1)} %bitcast.21, bf16[1024,128]{1,0:T(8,128)(2,1)S(1)} %copy-done, ...), custom_call_target="tpu_custom_call" | custom-call | tf_op jit(solution)/shard_map/pallas_call | solution.py:103
  60.0 0.7 copy-done.6
  60.7 3.4 %shard_map.99 = (f32[128,1024]{1,0:T(8,128)S(1)}, f32[512,128]{1,0:T(8,128)S(1)}) custom-call(f32[7,1024]{1,0:T(8,128)S(1)} %get-tuple-element.51.zt_ref, f32[7,1024]{1,0:T(8,128)S(1)} %get-tuple-element.50.zs_ref, bf16[1024,1024]{1,0:T(8,128)(2,1)S(1)} %bitcast.13, bf16[128,1024]{1,0:T(8,128)(2,1)S(1)} %bitcast.22, bf16[1024,128]{1,0:T(8,128)(2,1)S(1)} %copy-done, ...), custom_call_target="tpu_custom_call" | custom-call | tf_op jit(solution)/shard_map/pallas_call | solution.py:103
  64.2 1.3 %shard_map.100 = (f32[128,1024]{1,0:T(8,128)S(1)}, f32[256,128]{1,0:T(8,128)S(1)}) custom-call(f32[7,1024]{1,0:T(8,128)S(1)} %get-tuple-element.51.zt_ref, f32[7,1024]{1,0:T(8,128)S(1)} %get-tuple-element.50.zs_ref, bf16[1024,1024]{1,0:T(8,128)(2,1)S(1)} %bitcast.14, bf16[128,1024]{1,0:T(8,128)(2,1)S(1)} %bitcast.23, bf16[1024,128]{1,0:T(8,128)(2,1)S(1)} %copy-done, ...), custom_call_target="tpu_custom_call" | custom-call | tf_op jit(solution)/shard_map/pallas_call | solution.py:103
  65.5 2.7 %shard_map.101 = (f32[128,1024]{1,0:T(8,128)S(1)}, f32[256,128]{1,0:T(8,128)S(1)}) custom-call(f32[7,1024]{1,0:T(8,128)S(1)} %get-tuple-element.51.zt_ref, f32[7,1024]{1,0:T(8,128)S(1)} %get-tuple-element.50.zs_ref, bf16[1024,1024]{1,0:T(8,128)(2,1)S(1)} %bitcast.15, bf16[128,1024]{1,0:T(8,128)(2,1)S(1)} %bitcast.24, bf16[1024,128]{1,0:T(8,128)(2,1)S(1)} %copy-done, ...), custom_call_target="tpu_custom_call" | custom-call | tf_op jit(solution)/shard_map/pallas_call | solution.py:103
  68.3 1.0 pad_maximum_fusion
  69.3 0.5 collective-permute-start.7
  69.8 1.0 copy-done.5
  70.8 2.4 %shard_map.102 = (f32[128,1024]{1,0:T(8,128)S(1)}, f32[256,128]{1,0:T(8,128)S(1)}) custom-call(f32[7,1024]{1,0:T(8,128)S(1)} %get-tuple-element.51.zt_ref, f32[7,1024]{1,0:T(8,128)S(1)} %get-tuple-element.50.zs_ref, bf16[1024,1024]{1,0:T(8,128)(2,1)S(1)} %bitcast.16, bf16[128,1024]{1,0:T(8,128)(2,1)S(1)} %bitcast.25, bf16[1024,128]{1,0:T(8,128)(2,1)S(1)} %copy-done, ...), custom_call_target="tpu_custom_call" | custom-call | tf_op jit(solution)/shard_map/pallas_call | solution.py:103
  73.2 9.7 %collective-permute-start.17 = (f32[256,128]{1,0:T(8,128)S(1)}, f32[256,128]{1,0:T(8,128)S(1)}, u32[]{:S(2)}, u32[]{:S(2)}) collective-permute-start(f32[256,128]{1,0:T(8,128)S(1)} %get-tuple-element.36), channel_id=1, source_target_pairs={{0,252},{1,253},{2,254},{3,255},{4,8},{5,9},{6,10},{7,11},{8,4},{9... | collective-permute-start | bytes 393224 | tf_op jit(solution)/shard_map/ppermute | solution.py:141
  82.9 1.9 %shard_map.103 = (f32[128,1024]{1,0:T(8,128)S(1)}, f32[256,128]{1,0:T(8,128)}) custom-call(f32[7,1024]{1,0:T(8,128)S(1)} %get-tuple-element.51.zt_ref, f32[7,1024]{1,0:T(8,128)S(1)} %get-tuple-element.50.zs_ref, bf16[1024,1024]{1,0:T(8,128)(2,1)S(1)} %bitcast.17, bf16[128,1024]{1,0:T(8,128)(2,1)S(1)} %bitcast.26, bf16[1024,128]{1,0:T(8,128)(2,1)S(1)} %copy-done, ...), custom_call_target="tpu_custom_call" | custom-call | tf_op jit(solution)/shard_map/pallas_call | solution.py:103
  84.9 1.5 %collective-permute-start.18 = (f32[256,128]{1,0:T(8,128)}, f32[256,128]{1,0:T(8,128)S(1)}, u32[]{:S(2)}, u32[]{:S(2)}) collective-permute-start(f32[256,128]{1,0:T(8,128)} %get-tuple-element.37), channel_id=1, source_target_pairs={{0,254},{1,255},{2,252},{3,253},{4,10},{5,11},{6,8},{7,9},{8,6},{9... | collective-permute-start | bytes 393224 | tf_op jit(solution)/shard_map/ppermute | solution.py:141
  86.4 1.2 %slice_add_fusion.1 = (f32[512,128]{1,0:T(8,128)S(1)}, f32[512,128]{1,0:T(8,128)S(1)}) fusion(f32[1280,128]{1,0:T(8,128)} %collective-permute-done.12, f32[512,128]{1,0:T(8,128)S(1)} %get-tuple-element.29, f32[512,128]{1,0:T(8,128)} %collective-permute-done.11, f32[512,128]{1,0:T(8,128)S(1)} %copy-done.7), kind=kLoop, calls=%fused_computation.8 | loop fusion | flops 196608 | bytes 1835008 | tf_op jit(solution)/shard_map/add | solution.py:200
  87.6 0.1 collective-permute-start.14
  87.7 3.1 %collective-permute-start.15 = (f32[256,128]{1,0:T(8,128)S(1)}, f32[256,128]{1,0:T(8,128)S(1)}, u32[]{:S(2)}, u32[]{:S(2)}) collective-permute-start(f32[256,128]{1,0:T(8,128)S(1)} %get-tuple-element.49), channel_id=1, source_target_pairs={{0,4},{1,5},{2,6},{3,7},{4,0},{5,1},{6,2},{7,3},{8,12},{9,13},{10,... | collective-permute-start | bytes 393224 | tf_op jit(solution)/shard_map/ppermute | solution.py:141
  90.8 0.3 collective-permute-start.13
  91.1 0.9 slice_add_fusion.2
  92.0 2.3 %collective-permute-start.16 = (f32[256,128]{1,0:T(8,128)S(1)}, f32[256,128]{1,0:T(8,128)S(1)}, u32[]{:S(2)}, u32[]{:S(2)}) collective-permute-start(f32[256,128]{1,0:T(8,128)S(1)} %slice_add_fusion.2), channel_id=1, source_target_pairs={{0,253},{1,252},{2,255},{3,254},{4,9},{5,8},{6,11},{7,10},{8,5},{9... | collective-permute-start | bytes 393224 | tf_op jit(solution)/shard_map/ppermute | solution.py:141
  94.3 2.0 %copy.16 = f32[1024,128]{1,0:T(8,128)} copy(f32[1024,128]{0,1:T(8,128)} %bitcast.27) | data formatting | bytes 1048576
  96.3 2.7 %collective-permute-done.14 = f32[256,128]{1,0:T(8,128)S(1)} collective-permute-done((f32[256,128]{1,0:T(8,128)S(1)}, f32[256,128]{1,0:T(8,128)S(1)}, u32[]{:S(2)}, u32[]{:S(2)}) %collective-permute-start.14) | collective-permute-done | bytes 131104 | tf_op jit(solution)/shard_map/ppermute | solution.py:141
  99.1 3.7 %collective-permute-done.16 = f32[256,128]{1,0:T(8,128)S(1)} collective-permute-done((f32[256,128]{1,0:T(8,128)S(1)}, f32[256,128]{1,0:T(8,128)S(1)}, u32[]{:S(2)}, u32[]{:S(2)}) %collective-permute-start.16) | collective-permute-done | bytes 131104 | tf_op jit(solution)/shard_map/ppermute | solution.py:141
  102.8 1.6 %add_add_fusion = f32[256,128]{1,0:T(8,128)} fusion(f32[256,128]{1,0:T(8,128)S(1)} %collective-permute-done.18, f32[256,128]{1,0:T(8,128)} %copy-done.12, f32[256,128]{1,0:T(8,128)S(1)} %collective-permute-done.16, f32[256,128]{1,0:T(8,128)S(1)} %collective-permute-done.15, f32[256,128]{1,0:T(8,128)S(1)} %collective-permute-done.14, ...), kind=kLoop, calls=%fused_computation.10 | loop fusion | flops 196608 | bytes 1048580 | tf_op jit(solution)/shard_map/add | solution.py:215
  (63 shorter events, 0.5 us)
Async XLA Ops:
  0.6 6.3 %copy-start.10 = (bf16[512,1024]{1,0:T(8,128)(2,1)S(1)}, bf16[512,1024]{1,0:T(8,128)(2,1)}, u32[]{:S(2)}) copy-start(bf16[512,1024]{1,0:T(8,128)(2,1)} %param.9) | copy-start | bytes 3145732
  0.6 2.4 %copy-start.11 = (bf16[512,128]{1,0:T(8,128)(2,1)S(1)}, bf16[512,128]{1,0:T(8,128)(2,1)}, u32[]{:S(2)}) copy-start(bf16[512,128]{1,0:T(8,128)(2,1)} %param.11) | copy-start | bytes 393220
  3.7 46.4 %collective-permute-start.10 = (bf16[512,1152]{1,0:T(8,128)(2,1)}, bf16[512,1152]{1,0:T(8,128)(2,1)}, u32[]{:S(2)}, u32[]{:S(2)}) collective-permute-start(bf16[512,1152]{1,0:T(8,128)(2,1)} %constant_dynamic-update-slice_fusion.piece_ref), channel_id=1, source_target_pairs={{0,2},{1,3},{2,0},{3,1},{4,6},{5,7},{6,4},{7,5},{8,10},{9,11},{10,... | collective-permute-start | bytes 3538952 | tf_op jit(solution)/shard_map/ppermute | solution.py:141
  7.0 16.1 %collective-permute-start.4 = (bf16[512,1152]{1,0:T(8,128)(2,1)}, bf16[512,1152]{1,0:T(8,128)(2,1)S(1)}, u32[]{:S(2)}, u32[]{:S(2)}) collective-permute-start(bf16[512,1152]{1,0:T(8,128)(2,1)} %constant_dynamic-update-slice_fusion.piece_ref), channel_id=1, source_target_pairs={{0,250},{1,251},{2,8},{3,9},{4,254},{5,255},{6,12},{7,13},{8,2},{9... | collective-permute-start | bytes 3538952 | tf_op jit(solution)/shard_map/ppermute | solution.py:141
  7.0 3.1 %copy-start.15 = (s32[16,7]{0,1:T(8,128)S(1)}, s32[16,7]{0,1:T(8,128)}, u32[]{:S(2)}) copy-start(s32[16,7]{0,1:T(8,128)} %param.12) | copy-start | bytes 1348
  7.1 6.9 %collective-permute-start = (bf16[128,1152]{1,0:T(8,128)(2,1)S(1)}, bf16[128,1152]{1,0:T(8,128)(2,1)S(1)}, u32[]{:S(2)}, u32[]{:S(2)}) collective-permute-start(bf16[128,1152]{1,0:T(8,128)(2,1)S(1)} %get-tuple-element.46), channel_id=1, source_target_pairs={{0,5},{1,4},{2,7},{3,6},{4,1},{5,0},{6,3},{7,2},{8,13},{9,12},{10,... | collective-permute-start | bytes 884744 | tf_op jit(solution)/shard_map/ppermute | solution.py:141
  9.3 8.1 %collective-permute-start.2 = (bf16[128,1152]{1,0:T(8,128)(2,1)S(1)}, bf16[128,1152]{1,0:T(8,128)(2,1)S(1)}, u32[]{:S(2)}, u32[]{:S(2)}) collective-permute-start(bf16[128,1152]{1,0:T(8,128)(2,1)S(1)} %get-tuple-element.47), channel_id=1, source_target_pairs={{0,5},{1,4},{2,7},{3,6},{4,1},{5,0},{6,3},{7,2},{8,13},{9,12},{10,... | collective-permute-start | bytes 884744 | tf_op jit(solution)/shard_map/ppermute | solution.py:141
  14.0 16.4 %collective-permute-start.1 = (bf16[128,1152]{1,0:T(8,128)(2,1)S(1)}, bf16[128,1152]{1,0:T(8,128)(2,1)S(1)}, u32[]{:S(2)}, u32[]{:S(2)}) collective-permute-start(bf16[128,1152]{1,0:T(8,128)(2,1)S(1)} %collective-permute-done), channel_id=1, source_target_pairs={{0,1},{1,0},{2,3},{3,2},{4,5},{5,4},{6,7},{7,6},{8,9},{9,8},{10,11... | collective-permute-start | bytes 884744 | tf_op jit(solution)/shard_map/ppermute | solution.py:141
  17.4 13.7 %collective-permute-start.3 = (bf16[128,1152]{1,0:T(8,128)(2,1)S(1)}, bf16[128,1152]{1,0:T(8,128)(2,1)S(1)}, u32[]{:S(2)}, u32[]{:S(2)}) collective-permute-start(bf16[128,1152]{1,0:T(8,128)(2,1)S(1)} %collective-permute-done.2), channel_id=1, source_target_pairs={{0,1},{1,0},{2,3},{3,2},{4,5},{5,4},{6,7},{7,6},{8,9},{9,8},{10,11... | collective-permute-start | bytes 884744 | tf_op jit(solution)/shard_map/ppermute | solution.py:141
  18.9 13.2 %copy-start.13 = (f32[4,1024]{1,0:T(4,128)S(1)}, f32[4,1024]{1,0:T(4,128)}, u32[]{:S(2)}) copy-start(f32[4,1024]{1,0:T(4,128)} %param.15) | copy-start | bytes 49156
  18.9 13.2 %copy-start.14 = (f32[4,1024]{1,0:T(4,128)S(1)}, f32[4,1024]{1,0:T(4,128)}, u32[]{:S(2)}) copy-start(f32[4,1024]{1,0:T(4,128)} %param.14) | copy-start | bytes 49156
  18.9 13.2 %copy-start.16 = (s32[1024]{0:T(1024)S(1)}, s32[1024]{0:T(1024)}, u32[]{:S(2)}) copy-start(s32[1024]{0:T(1024)} %param.13) | copy-start | bytes 12292
  23.1 8.0 %copy-start.1 = (bf16[512,1152]{1,0:T(8,128)(2,1)}, bf16[512,1152]{1,0:T(8,128)(2,1)S(1)}, u32[]{:S(2)}) copy-start(bf16[512,1152]{1,0:T(8,128)(2,1)S(1)} %collective-permute-done.4.piece_ref) | copy-start | bytes 3538948
  23.3 14.9 %collective-permute-start.5 = (bf16[256,1152]{1,0:T(8,128)(2,1)S(1)}, bf16[256,1152]{1,0:T(8,128)(2,1)S(1)}, u32[]{:S(2)}, u32[]{:S(2)}) collective-permute-start(bf16[256,1152]{1,0:T(8,128)(2,1)S(1)} %maximum_select_fusion.1), channel_id=1, source_target_pairs={{0,8},{1,9},{2,5},{3,4},{4,3},{5,2},{6,254},{7,255},{8,16},{9,17},... | collective-permute-start | bytes 1769480 | tf_op jit(solution)/shard_map/ppermute | solution.py:141
  31.9 28.9 %collective-permute-start.9 = (bf16[512,1152]{1,0:T(8,128)(2,1)}, bf16[512,1152]{1,0:T(8,128)(2,1)}, u32[]{:S(2)}, u32[]{:S(2)}) collective-permute-start(bf16[512,1152]{1,0:T(8,128)(2,1)} %constant_dynamic-update-slice_fusion.2.piece_ref), channel_id=1, source_target_pairs={{0,2},{1,3},{2,0},{3,1},{4,6},{5,7},{6,4},{7,5},{8,10},{9,11},{10,... | collective-permute-start | bytes 3538952 | tf_op jit(solution)/shard_map/ppermute | solution.py:141
  38.2 27.3 %collective-permute-start.8 = (bf16[256,1152]{1,0:T(8,128)(2,1)S(1)}, bf16[256,1152]{1,0:T(8,128)(2,1)}, u32[]{:S(2)}, u32[]{:S(2)}) collective-permute-start(bf16[256,1152]{1,0:T(8,128)(2,1)S(1)} %collective-permute-done.5.piece_ref), channel_id=1, source_target_pairs={{0,2},{1,3},{2,0},{3,1},{4,6},{5,7},{6,4},{7,5},{8,10},{9,11},{10,... | collective-permute-start | bytes 1769480 | tf_op jit(solution)/shard_map/ppermute | solution.py:141
  41.9 27.4 %collective-permute-start.6 = (bf16[256,1152]{1,0:T(8,128)(2,1)}, bf16[256,1152]{1,0:T(8,128)(2,1)}, u32[]{:S(2)}, u32[]{:S(2)}) collective-permute-start(bf16[256,1152]{1,0:T(8,128)(2,1)} %maximum_select_fusion), channel_id=1, source_target_pairs={{0,8},{1,9},{2,3},{3,2},{4,5},{5,4},{6,254},{7,255},{8,16},{9,17},... | collective-permute-start | bytes 1769480 | tf_op jit(solution)/shard_map/ppermute | solution.py:141
  43.5 3.1 %copy-start = (bf16[1024,128]{1,0:T(8,128)(2,1)S(1)}, bf16[1024,128]{1,0:T(8,128)(2,1)}, u32[]{:S(2)}) copy-start(bf16[1024,128]{1,0:T(8,128)(2,1)} %sq_ref.17) | copy-start | bytes 786436
  50.2 3.5 %copy-start.2 = (bf16[512,1152]{1,0:T(8,128)(2,1)S(1)}, bf16[512,1152]{1,0:T(8,128)(2,1)}, u32[]{:S(2)}) copy-start(bf16[512,1152]{1,0:T(8,128)(2,1)} %copy-done.1) | copy-start | bytes 3538948
  60.0 0.7 copy-start.6
  65.5 2.7 %copy-start.8 = (f32[256,128]{1,0:T(8,128)}, f32[256,128]{1,0:T(8,128)S(1)}, u32[]{:S(2)}) copy-start(f32[256,128]{1,0:T(8,128)S(1)} %get-tuple-element.35) | copy-start | bytes 393220
  68.3 1.0 copy-start.4
  69.3 17.1 %collective-permute-start.12 = (f32[1280,128]{1,0:T(8,128)}, f32[1280,128]{1,0:T(8,128)}, u32[]{:S(2)}, u32[]{:S(2)}) collective-permute-start(f32[1280,128]{1,0:T(8,128)} %pad_maximum_fusion), channel_id=1, source_target_pairs={{0,2},{1,3},{2,0},{3,1},{4,6},{5,7},{6,4},{7,5},{8,10},{9,11},{10,... | collective-permute-start | bytes 1966088 | tf_op jit(solution)/shard_map/ppermute | solution.py:141
  69.3 13.7 %collective-permute-start.7 = (bf16[256,1152]{1,0:T(8,128)(2,1)}, bf16[256,1152]{1,0:T(8,128)(2,1)S(1)}, u32[]{:S(2)}, u32[]{:S(2)}) collective-permute-start(bf16[256,1152]{1,0:T(8,128)(2,1)} %collective-permute-done.6.piece_ref), channel_id=1, source_target_pairs={{0,2},{1,3},{2,0},{3,1},{4,6},{5,7},{6,4},{7,5},{8,10},{9,11},{10,... | collective-permute-start | bytes 1769480 | tf_op jit(solution)/shard_map/ppermute | solution.py:141
  69.8 16.6 %collective-permute-start.11 = (f32[512,128]{1,0:T(8,128)}, f32[512,128]{1,0:T(8,128)}, u32[]{:S(2)}, u32[]{:S(2)}) collective-permute-start(f32[512,128]{1,0:T(8,128)} %get-tuple-element.30), channel_id=1, source_target_pairs={{0,250},{1,251},{2,8},{3,9},{4,254},{5,255},{6,12},{7,13},{8,2},{9... | collective-permute-start | bytes 786440 | tf_op jit(solution)/shard_map/ppermute | solution.py:141
  69.8 1.0 copy-start.5
  73.2 18.8 %collective-permute-start.17 = (f32[256,128]{1,0:T(8,128)S(1)}, f32[256,128]{1,0:T(8,128)S(1)}, u32[]{:S(2)}, u32[]{:S(2)}) collective-permute-start(f32[256,128]{1,0:T(8,128)S(1)} %get-tuple-element.36), channel_id=1, source_target_pairs={{0,252},{1,253},{2,254},{3,255},{4,8},{5,9},{6,10},{7,11},{8,4},{9... | collective-permute-start | bytes 393224 | tf_op jit(solution)/shard_map/ppermute | solution.py:141
  82.9 3.4 %copy-start.7 = (f32[512,128]{1,0:T(8,128)S(1)}, f32[512,128]{1,0:T(8,128)}, u32[]{:S(2)}) copy-start(f32[512,128]{1,0:T(8,128)} %copy-done.6) | copy-start | bytes 786436
  84.9 2.7 %copy-start.3 = (f32[128,1024]{1,0:T(8,128)}, f32[128,1024]{1,0:T(8,128)S(1)}, u32[]{:S(2)}) copy-start(f32[128,1024]{1,0:T(8,128)S(1)} %get-tuple-element.28) | copy-start | bytes 1572868
  84.9 11.5 %collective-permute-start.18 = (f32[256,128]{1,0:T(8,128)}, f32[256,128]{1,0:T(8,128)S(1)}, u32[]{:S(2)}, u32[]{:S(2)}) collective-permute-start(f32[256,128]{1,0:T(8,128)} %get-tuple-element.37), channel_id=1, source_target_pairs={{0,254},{1,255},{2,252},{3,253},{4,10},{5,11},{6,8},{7,9},{8,6},{9... | collective-permute-start | bytes 393224 | tf_op jit(solution)/shard_map/ppermute | solution.py:141
  86.4 4.7 %copy-start.9 = (f32[256,128]{1,0:T(8,128)S(1)}, f32[256,128]{1,0:T(8,128)}, u32[]{:S(2)}) copy-start(f32[256,128]{1,0:T(8,128)} %copy-done.8) | copy-start | bytes 393220
  87.6 11.4 %collective-permute-start.14 = (f32[256,128]{1,0:T(8,128)S(1)}, f32[256,128]{1,0:T(8,128)S(1)}, u32[]{:S(2)}, u32[]{:S(2)}) collective-permute-start(f32[256,128]{1,0:T(8,128)S(1)} %get-tuple-element.48), channel_id=1, source_target_pairs={{0,5},{1,4},{2,7},{3,6},{4,1},{5,0},{6,3},{7,2},{8,13},{9,12},{10,... | collective-permute-start | bytes 393224 | tf_op jit(solution)/shard_map/ppermute | solution.py:141
  87.7 11.3 %collective-permute-start.15 = (f32[256,128]{1,0:T(8,128)S(1)}, f32[256,128]{1,0:T(8,128)S(1)}, u32[]{:S(2)}, u32[]{:S(2)}) collective-permute-start(f32[256,128]{1,0:T(8,128)S(1)} %get-tuple-element.49), channel_id=1, source_target_pairs={{0,4},{1,5},{2,6},{3,7},{4,0},{5,1},{6,2},{7,3},{8,12},{9,13},{10,... | collective-permute-start | bytes 393224 | tf_op jit(solution)/shard_map/ppermute | solution.py:141
  90.8 8.3 %collective-permute-start.13 = (f32[256,128]{1,0:T(8,128)S(1)}, f32[256,128]{1,0:T(8,128)S(1)}, u32[]{:S(2)}, u32[]{:S(2)}) collective-permute-start(f32[256,128]{1,0:T(8,128)S(1)} %constant_dynamic-slice_fusion), channel_id=1, source_target_pairs={{0,1},{1,0},{2,3},{3,2},{4,5},{5,4},{6,7},{7,6},{8,9},{9,8},{10,11... | collective-permute-start | bytes 393224 | tf_op jit(solution)/shard_map/ppermute | solution.py:141
  92.0 2.3 %copy-start.12 = (f32[256,128]{1,0:T(8,128)}, f32[256,128]{1,0:T(8,128)S(1)}, u32[]{:S(2)}) copy-start(f32[256,128]{1,0:T(8,128)S(1)} %collective-permute-done.17) | copy-start | bytes 393220
  92.0 10.8 %collective-permute-start.16 = (f32[256,128]{1,0:T(8,128)S(1)}, f32[256,128]{1,0:T(8,128)S(1)}, u32[]{:S(2)}, u32[]{:S(2)}) collective-permute-start(f32[256,128]{1,0:T(8,128)S(1)} %slice_add_fusion.2), channel_id=1, source_target_pairs={{0,253},{1,252},{2,255},{3,254},{4,9},{5,8},{6,11},{7,10},{8,5},{9... | collective-permute-start | bytes 393224 | tf_op jit(solution)/shard_map/ppermute | solution.py:141

commit v2 on v1

v2 whole, which is shorter than its diff:
```python
import functools
import math

import jax
import jax.numpy as jnp
from jax import lax
from jax.experimental import pallas as pl
from jax.experimental.pallas import tpu as pltpu
from jax.sharding import PartitionSpec as P

logit_cap = 10.0
score_gain = 3.0
loss_weight = 8.0
log2e = 1.0 / math.log(2.0)
never = 1e9
long_cost = 10**10
AXES = ("items", "rep")


def edges(n_items, move):
    pairs = []
    for flat in range(n_items * 2):
        item, rep = flat // 2, flat % 2
        pos, y, core = item // 4, (item // 2 % 2) * 2 + rep, item % 2
        pos, y, core = move(pos, y, core)
        pos = pos % (n_items // 4)
        target = ((pos * 2 + y // 2) * 2 + core) * 2 + y % 2
        pairs.append((flat, target))
    return pairs


def step(y):
    return -1 if y < 2 else 1


def far(p, y, c):
    return (p + 1, y, 0) if c == 1 else (p - 1, y, 1)


def cross(p, y, c):
    return p, 3 - y, c


def pair(p, y, c):
    return p, y ^ 1, c


def two(p, y, c):
    return p, y ^ 2, c


def core(p, y, c):
    return p, y, 1 - c


def diag(p, y, c):
    return p + step(y), 3 - y, c


def diag_two(p, y, c):
    return p + step(y), y ^ 2, c


def far_pair(p, y, c):
    p, y, c = far(p, y, c)
    return p, y ^ 1, c


def gather_kernel(rep_ref, teacher_ref, student_ref, out_ref, sems):
    rows = out_ref.shape[0]
    part = pl.ds(pl.multiple_of(rep_ref[0] * rows, rows), rows)
    copies = []
    for source, first in ((teacher_ref, 0), (student_ref, teacher_ref.shape[1])):
        target = out_ref.at[:, pl.ds(first, source.shape[1])]
        copies.append(pltpu.make_async_copy(source.at[part, :], target, sems.at[len(copies)]))
    for copy in copies:
        copy.start()
    for copy in copies:
        copy.wait()


def gather(rep, teacher, student):
    rows, width = teacher.shape[0] // 2, teacher.shape[1] + student.shape[1]
    whole = pl.BlockSpec(memory_space=pl.ANY)
    return pl.pallas_call(
        gather_kernel,
        out_shape=jax.ShapeDtypeStruct((rows, width), teacher.dtype),
        in_specs=[pl.BlockSpec(memory_space=pltpu.SMEM), whole, whole],
        out_specs=pl.BlockSpec(memory_space=pltpu.VMEM),
        scratch_shapes=[pltpu.SemaphoreType.DMA((2,))],
        compiler_params=pltpu.CompilerParams(vmem_limit_bytes=56 << 20),
        cost_estimate=pl.CostEstimate(flops=1, bytes_accessed=1, transcendentals=0),
    )(rep, teacher, student)


def turn_kernel(tq_ref, sq_ref, tqt_ref, sqt_ref):
    rows = 256
    for start in range(0, tq_ref.shape[0], rows):
        tqt_ref[:, start : start + rows] = tq_ref[start : start + rows, :].T
        sqt_ref[:, start : start + rows] = sq_ref[start : start + rows, :].T


def turn(tq, sq):
    vmem = pl.BlockSpec(memory_space=pltpu.VMEM)
    return pl.pallas_call(
        turn_kernel,
        out_shape=tuple(pltpu.VMEM(block.shape[::-1], block.dtype) for block in (tq, sq)),
        in_specs=[vmem] * 2,
        out_specs=(vmem,) * 2,
        compiler_params=pltpu.CompilerParams(vmem_limit_bytes=16 << 20),
        cost_estimate=pl.CostEstimate(flops=1, bytes_accessed=1, transcendentals=0),
    )(tq, sq)


def visit_kernel(parts, rows, first, scales, rep_ref, *refs):
    groups = len(rows)
    term_ref = refs[-1]
    if parts is None:
        width = refs[0].shape[1] - term_ref.shape[1]
        teacher, student = refs[0][:, :width], refs[0][:, width:]
        refs = refs[1:]
    else:
        half = refs[0].shape[0] // 2
        rep = rep_ref[0]
        picks = [pl.ds(pl.multiple_of((1 - rep if part else rep) * half, half), half) for part in parts]
        teacher, student = (
            jnp.concatenate([ref[pick, :] for pick in picks]) if len(picks) > 1 else ref[picks[0], :]
            for ref in refs[:2]
        )
        refs = refs[2:]
    term = None
    for group, row in enumerate(rows):
        zt_ref, zs_ref, tqt_ref, sqt_ref, sq_ref = refs[group * 5 : group * 5 + 5]
        t_raw = jnp.dot(teacher, tqt_ref[...], preferred_element_type=jnp.float32)
        s_raw = jnp.dot(student, sqt_ref[...], preferred_element_type=jnp.float32)
        t_tanh = jnp.tanh(t_raw * scales[0])
        s_tanh = jnp.tanh(s_raw * scales[1])
        t_exp = jnp.exp2(t_tanh * (logit_cap * log2e) - zt_ref[row : row + 1, :])
        s_exp = jnp.exp2(s_tanh * (logit_cap * log2e) - zs_ref[row : row + 1, :])
        grads = ((s_exp - t_exp) * (1.0 - s_tanh * s_tanh)).astype(jnp.bfloat16)
        part = jnp.dot(grads, sq_ref[...], preferred_element_type=jnp.float32)
        term = part if term is None else term + part
        q_part = lax.dot_general(
            student, grads, (((0,), (0,)), ((), ())), preferred_element_type=jnp.float32
        )
        q_ref = refs[-1 - groups + group]
        q_ref[...] = q_part if first else refs[groups * 5 + group][...] + q_part
    term_ref[...] = term


def visit(rep, piece, parts, rows, groups, scales, totals, cost=1):
    width, requests = groups[0][3].shape
    vmem = pl.BlockSpec(memory_space=pltpu.VMEM)
    items = piece[0].shape[0] if parts is None else piece[0].shape[0] // 2 * len(parts)
    operands = [*piece]
    for group in groups:
        operands.extend(group)
    operands.extend(totals)
    *totals, term = pl.pallas_call(
        functools.partial(visit_kernel, parts, rows, not totals, scales),
        out_shape=tuple([jax.ShapeDtypeStruct((width, requests), jnp.float32)] * len(groups))
        + (jax.ShapeDtypeStruct((items, width), jnp.float32),),
        in_specs=[pl.BlockSpec(memory_space=pltpu.SMEM)] + [vmem] * len(operands),
        out_specs=(vmem,) * (len(groups) + 1),
        compiler_params=pltpu.CompilerParams(vmem_limit_bytes=24 << 20),
        cost_estimate=pl.CostEstimate(flops=cost, bytes_accessed=1, transcendentals=0),
    )(rep, *operands)
    return totals, term


def shards(
    teacher_queries,
    teacher_items,
    student_queries,
    student_items,
    block_mask,
    pass_index,
    teacher_norms,
    student_norms,
):
    n_items = lax.axis_size("items")
    rows = teacher_queries.shape[0]
    blocks = block_mask.shape[0]
    span = teacher_items.shape[0]
    half = span // 2
    teacher_scale = score_gain / math.sqrt(teacher_queries.shape[1])
    student_scale = score_gain / math.sqrt(student_queries.shape[1])
    scales = (teacher_scale / logit_cap, student_scale / logit_cap)

    item = lax.axis_index("items")
    rep = lax.axis_index("rep")
    core_id = item % 2
    type_b = item // 2 % 2

    def send(block, move):
        return lax.ppermute(block, AXES, edges(n_items, move))

    def stage(*blocks):
        return lax.optimization_barrier(blocks)

    where = jnp.reshape(rep, (1,)).astype(jnp.int32)
    diag_half = send(gather(where, teacher_items, student_items), diag)
    own = (teacher_items, student_items)
    far_span = [send(block, far) for block in own]
    across = [send(block, cross) for block in own]
    other_tq = send(teacher_queries, core)
    other_sq = send(student_queries, core)

    passes = jnp.arange(teacher_norms.shape[0], dtype=jnp.int32)
    picked = (pass_index[None, :] == passes[:, None]).astype(jnp.float32)
    fold = math.log2(loss_weight * student_scale)
    zt = jnp.sum(teacher_norms * picked, axis=0) * log2e - fold
    zs = jnp.sum(student_norms * picked, axis=0) * log2e - fold
    near = 1 - 2 * core_id
    ahead = 2 - 4 * type_b
    offsets = jnp.stack([0 * near, ahead, -ahead, -3 * near, near, ahead + near, near - ahead])
    reach = block_mask.shape[1] // 2
    chosen = offsets[:, None, None] + reach == jnp.arange(2 * reach + 1)[None, None, :]
    on = jnp.any(chosen & (block_mask[None] != 0), axis=2)
    on = jnp.broadcast_to(on[:, :, None], (on.shape[0], blocks, rows // blocks))
    on = on.reshape(on.shape[0], rows)
    zt_all = jnp.where(on, zt[None], never)
    zs_all = jnp.where(on, zs[None], never)
    other_z = send(jnp.concatenate([zt_all[3:], zs_all[3:]]), core)
    mine = (zt_all, zs_all, *turn(teacher_queries, student_queries), student_queries)
    other = (other_z[:4], other_z[4:], *turn(other_tq, other_sq), other_sq)
    both = (mine, other)
    q, own_term = visit(where, own, (0, 1), (0, 1), both, scales, [])

    diag_half, q, own_term = stage(diag_half, q, own_term)
    next_half = send(diag_half, pair)
    q, diag_term = visit(where, [diag_half], None, (2, 3), both, scales, q, cost=long_cost)
    diag_back = send(diag_term, diag)

    far_span, next_half, q, own_term, diag_back = stage(far_span, next_half, q, own_term, diag_back)
    q[:1], far_term = visit(where, far_span, (0, 1), (3,), both[:1], scales, q[:1])
    pair_back = send(jnp.concatenate([own_term[half:], far_term[half:]]), pair)
    q, next_term = visit(where, [next_half], None, (2, 3), both, scales, q)
    next_back = send(next_term, diag_two)

    across, q, own_term, far_term, next_back = stage(across, q, own_term, far_term, next_back)
    q, first_term = visit(where, across, (1,), (1, 2), both, scales, q)
    cross_back = send(first_term, cross)
    far_back = send(far_term[:half] + pair_back[half:], far)
    q, last_term = visit(where, across, (0,), (1, 2), both, scales, q, cost=long_cost)
    q = q[0] + send(q[1], core)
    last_back = send(last_term, two)
    total = own_term[:half] + pair_back[:half] + diag_back + next_back
    return q.T, total + cross_back + far_back + last_back


def solution(mesh):
    return jax.shard_map(
        shards,
        mesh=mesh,
        in_specs=(
            P(("items", "rep"), None),
            P("items", None),
            P(("items", "rep"), None),
            P("items", None),
            P(("items", "rep"), None),
            P(("items", "rep")),
            P(None, ("items", "rep")),
            P(None, ("items", "rep")),
        ),
        out_specs=(P(("items", "rep"), None), P(("items", "rep"), None)),
        check_vma=False,
    )
```

time: 105 us -> 77 us (0.73)
  waiting for transfers between devices: 24 us -> 10.6 us
  local copies, waits for them, and re-layouts: 13.5 us -> 2.9 us
  other arithmetic: 6.09 us -> 2.48 us
  Pallas kernels: 25 us -> 22.3 us
  starting transfers between devices: 34.8 us -> 37.1 us
    ppermute x19 -> x16, waiting for transfers between devices: 24 us -> 10.6 us  [send(): return lax.ppermute(block, AXES, edges(n_items, move))]
    unnamed x41 -> x9, local copies, waits for them, and re-layouts: 11.7 us -> 2.59 us
    add x3 -> x2, other arithmetic: 3.73 us -> 0.73 us  [the longest x1 0.71 us: shards(): return (q.T, total + cross_back + far_back + last_back)]
    pallas_call x9, Pallas kernels: 25 us -> 22.3 us  [the longest x6 17.4 us: visit(): pl.pallas_call(functools.partial(visit_kernel, parts, rows, not totals, s...]
    ppermute x19 -> x16, starting transfers between devices: 34.8 us -> 37.1 us  [send(): return lax.ppermute(block, AXES, edges(n_items, move))]
    concatenate x2 -> x0, local copies, waits for them, and re-layouts: 1.44 us -> none  [the longest x1 0.75 us: shards(): across = jnp.concatenate([cross_half, pair_half])]
    select_n x3 -> x1, other arithmetic: 1.11 us -> 0.01 us  [shards(): zs_all = jnp.where(on, zs[None], never)]
  transfers between devices with their start and end apart: 19 -> 16, of which waited for: 6 -> 4; matrix products, arithmetic and copies ran while one was open for 13% -> 4% of each run, Pallas kernels for 24% -> 29%
where the time goes in v2:
time: 77 us; the launch traced here: 76.3 us
  starting transfers between devices  37.1 us (48%)
  Pallas kernels  22.3 us (29%)
  waiting for transfers between devices  10.6 us (14%)
  local copies, waits for them, and re-layouts  2.9 us (4%)
  other arithmetic  2.48 us (3%)
  between operations  0.92 us (1%)
    ppermute x16, starting transfers between devices, send(): return lax.ppermute(block, AXES, edges(n_items, move))  37.1 us
    pallas_call x6, Pallas kernels, visit(): pl.pallas_call(functools.partial(visit_kernel, parts, rows, not totals, s...  17.4 us
    ppermute x16, waiting for transfers between devices, send(): return lax.ppermute(block, AXES, edges(n_items, move))  10.6 us
    pallas_call x2, Pallas kernels, turn(): pl.pallas_call(turn_kernel, out_shape=tuple((pltpu.VMEM(block.shape[::-1]...  3 us
    unnamed x9, local copies, waits for them, and re-layouts  2.59 us
    pallas_call x1, Pallas kernels, gather(): pl.pallas_call(gather_kernel, out_shape=jax.ShapeDtypeStruct((rows, width...  1.91 us
  transfers between devices with their start and end apart: 16, of which 4 were waited for; matrix products, arithmetic and copies ran while one was open for 4% of the time, Pallas kernels for 29%

profile of v2, /device:TPU:1, one launch (start us, length us, event | category | flops | bytes accessed | tf_op | source)
XLA Modules:
  0.0 76.3 jit_solution(15375304982063713514)
XLA Ops:
  0.7 3.3 %collective-permute-start.6 = (bf16[1024,1024]{1,0:T(8,128)(2,1)}, bf16[1024,1024]{1,0:T(8,128)(2,1)}, u32[]{:S(2)}, u32[]{:S(2)}) collective-permute-start(bf16[1024,1024]{1,0:T(8,128)(2,1)} %tq_ref.1), channel_id=1, source_target_pairs={{0,2},{1,3},{2,0},{3,1},{4,6},{5,7},{6,4},{7,5},{8,10},{9,11},{10,... | collective-permute-start | bytes 6291464 | tf_op jit(solution)/shard_map/ppermute | solution.py:196
  4.0 0.1 collective-permute-start.7
  4.1 1.9 %shard_map.95 = bf16[256,1152]{1,0:T(8,128)(2,1)} custom-call(s32[1]{0:T(128)} %bitcast.rep_ref, bf16[512,1024]{1,0:T(8,128)(2,1)} %refs_0_.1, bf16[512,128]{1,0:T(8,128)(2,1)} %refs_1_.1), custom_call_target="tpu_custom_call" | custom-call | flops 1 | bytes 1 | tf_op jit(solution)/shard_map/pallas_call | solution.py:85
  6.0 8.6 %collective-permute-start.4 = (bf16[256,1152]{1,0:T(8,128)(2,1)}, bf16[256,1152]{1,0:T(8,128)(2,1)S(1)}, u32[]{:S(2)}, u32[]{:S(2)}) collective-permute-start(bf16[256,1152]{1,0:T(8,128)(2,1)} %shard_map.95), channel_id=1, source_target_pairs={{0,253},{1,252},{2,255},{3,254},{4,9},{5,8},{6,11},{7,10},{8,5},{9... | collective-permute-start | bytes 1769480 | tf_op jit(solution)/shard_map/ppermute | solution.py:196
  14.6 0.1 stack.27
  14.7 0.1 iota_compare_fusion.1
  14.7 0.7 broadcast_compare_fusion
  15.4 0.1 and_reduce_fusion
  15.5 0.1 broadcast_in_dim.31
  15.6 0.1 reshape.101
  15.7 0.8 %select_reduce_fusion = (f32[1024]{0:T(1024)S(1)}, f32[1024]{0:T(1024)S(1)}) fusion(f32[4,1024]{1,0:T(4,128)} %param.15, s32[1024]{0:T(1024)} %param.13, f32[4,1024]{1,0:T(4,128)} %param.14), kind=kLoop, calls=%fused_computation.12 | loop fusion | flops 18432 | bytes 45056 | tf_op jit(solution)/shard_map/reduce_sum | solution.py:213
  16.6 0.8 %collective-permute-start.5 = (f32[8,1024]{1,0:T(8,128)S(1)}, f32[8,1024]{1,0:T(8,128)S(1)}, u32[]{:S(2)}, u32[]{:S(2)}) collective-permute-start(f32[8,1024]{1,0:T(8,128)S(1)} %pad_maximum_fusion.1), channel_id=1, source_target_pairs={{0,2},{1,3},{2,0},{3,1},{4,6},{5,7},{6,4},{7,5},{8,10},{9,11},{10,... | collective-permute-start | bytes 98312 | tf_op jit(solution)/shard_map/ppermute | solution.py:196
  17.4 0.0 collective-permute-start.2
  17.4 0.0 copy-start.2
  17.4 1.6 %copy-done.2 = bf16[1024,1024]{1,0:T(8,128)(2,1)S(1)} copy-done((bf16[1024,1024]{1,0:T(8,128)(2,1)S(1)}, bf16[1024,1024]{1,0:T(8,128)(2,1)}, u32[]{:S(2)}) %copy-start.2) | copy-done | bytes 2097176
  19.0 0.7 shard_map.96
  19.7 0.0 collective-permute-done.5
  19.7 1.8 %collective-permute-start.3 = (bf16[512,128]{1,0:T(8,128)(2,1)S(1)}, bf16[512,128]{1,0:T(8,128)(2,1)S(1)}, u32[]{:S(2)}, u32[]{:S(2)}) collective-permute-start(bf16[512,128]{1,0:T(8,128)(2,1)S(1)} %copy-done.3), channel_id=1, source_target_pairs={{0,250},{1,251},{2,8},{3,9},{4,254},{5,255},{6,12},{7,13},{8,2},{9... | collective-permute-start | bytes 393224 | tf_op jit(solution)/shard_map/ppermute | solution.py:196
  21.5 0.0 collective-permute-done.7.sq_ref.refs_11_.refs_10_
  21.5 0.1 collective-permute-start
  21.6 0.0 collective-permute-done.6.tq_ref
  21.7 2.3 %shard_map.97 = (bf16[1024,1024]{1,0:T(8,128)(2,1)S(1)}, bf16[128,1024]{1,0:T(8,128)(2,1)S(1)}) custom-call(bf16[1024,1024]{1,0:T(8,128)(2,1)} %collective-permute-done.6.tq_ref, bf16[1024,128]{1,0:T(8,128)(2,1)S(1)} %collective-permute-done.7.sq_ref.refs_11_.refs_10_), custom_call_target="tpu_custom_call" | custom-call | flops 1 | bytes 1 | tf_op jit(solution)/shard_map/pallas_call | solution.py:105
  24.0 4.7 %shard_map.98 = (f32[128,1024]{1,0:T(8,128)S(1)}, f32[128,1024]{1,0:T(8,128)S(1)}, f32[512,128]{1,0:T(8,128)S(1)}) custom-call(s32[1]{0:T(128)} %bitcast.rep_ref, bf16[512,1024]{1,0:T(8,128)(2,1)S(1)} %copy-done.1, bf16[512,128]{1,0:T(8,128)(2,1)S(1)} %copy-done.3, f32[7,1024]{1,0:T(8,128)S(1)} %get-tuple-element.89.refs_2_.refs_1_, ...), custom_call_target="tpu_custom_call" | custom-call | flops 1 | bytes 1 | tf_op jit(solution)/shard_map/pallas_call | solution.py:159
  28.6 0.3 collective-permute-start.8
  28.9 2.6 %shard_map.99 = (f32[128,1024]{1,0:T(8,128)S(1)}, f32[128,1024]{1,0:T(8,128)S(1)}, f32[256,128]{1,0:T(8,128)S(1)}) custom-call(s32[1]{0:T(128)} %bitcast.rep_ref, bf16[256,1152]{1,0:T(8,128)(2,1)S(1)} %collective-permute-done.4.refs_0_, f32[7,1024]{1,0:T(8,128)S(1)} %get-tuple-element.89.refs_2_.refs_1_, f32[7,1024]{1,0:T(8,128)S(1)} %get-tuple-element.88.refs_3_.refs_2_, ...), custom_call_target="tpu_custom_call" | custom-call | flops 10000000000 | bytes 1 | tf_op jit(solution)/shard_map/pallas_call | solution.py:159
  31.6 6.3 %collective-permute-start.9 = (f32[256,128]{1,0:T(8,128)S(1)}, f32[256,128]{1,0:T(8,128)S(1)}, u32[]{:S(2)}, u32[]{:S(2)}) collective-permute-start(f32[256,128]{1,0:T(8,128)S(1)} %get-tuple-element.54), channel_id=1, source_target_pairs={{0,253},{1,252},{2,255},{3,254},{4,9},{5,8},{6,11},{7,10},{8,5},{9... | collective-permute-start | bytes 393224 | tf_op jit(solution)/shard_map/ppermute | solution.py:196
  37.9 0.0 collective-permute-done.3.refs_1_
  37.9 0.0 collective-permute-start.1
  37.9 0.0 collective-permute-done.2.refs_0_
  37.9 4.6 %collective-permute-done.9 = f32[256,128]{1,0:T(8,128)S(1)} collective-permute-done((f32[256,128]{1,0:T(8,128)S(1)}, f32[256,128]{1,0:T(8,128)S(1)}, u32[]{:S(2)}, u32[]{:S(2)}) %collective-permute-start.9) | collective-permute-done | bytes 131104 | tf_op jit(solution)/shard_map/ppermute | solution.py:196
  42.5 0.0 collective-permute-done.8.refs_0_
  42.5 2.2 %shard_map.100 = (f32[128,1024]{1,0:T(8,128)S(1)}, f32[512,128]{1,0:T(8,128)S(1)}) custom-call(s32[1]{0:T(128)} %bitcast.rep_ref, bf16[512,1024]{1,0:T(8,128)(2,1)S(1)} %collective-permute-done.2.refs_0_, bf16[512,128]{1,0:T(8,128)(2,1)S(1)} %collective-permute-done.3.refs_1_, f32[7,1024]{1,0:T(8,128)S(1)} %get-tuple-element.89.refs_2_.refs_1_, ...), custom_call_target="tpu_custom_call" | custom-call | flops 1 | bytes 1 | tf_op jit(solution)/shard_map/pallas_call | solution.py:159
  44.7 2.6 %shard_map.101 = (f32[128,1024]{1,0:T(8,128)S(1)}, f32[128,1024]{1,0:T(8,128)S(1)}, f32[256,128]{1,0:T(8,128)S(1)}) custom-call(s32[1]{0:T(128)} %bitcast.rep_ref, bf16[256,1152]{1,0:T(8,128)(2,1)S(1)} %collective-permute-done.8.refs_0_, f32[7,1024]{1,0:T(8,128)S(1)} %get-tuple-element.89.refs_2_.refs_1_, f32[7,1024]{1,0:T(8,128)S(1)} %get-tuple-element.88.refs_3_.refs_2_, ...), custom_call_target="tpu_custom_call" | custom-call | flops 1 | bytes 1 | tf_op jit(solution)/shard_map/pallas_call | solution.py:159
  47.3 6.7 %collective-permute-start.10 = (f32[256,128]{1,0:T(8,128)S(1)}, f32[256,128]{1,0:T(8,128)S(1)}, u32[]{:S(2)}, u32[]{:S(2)}) collective-permute-start(f32[256,128]{1,0:T(8,128)S(1)} %get-tuple-element.65), channel_id=1, source_target_pairs={{0,252},{1,253},{2,254},{3,255},{4,8},{5,9},{6,10},{7,11},{8,4},{9... | collective-permute-start | bytes 393224 | tf_op jit(solution)/shard_map/ppermute | solution.py:196
  54.1 1.4 %collective-permute-start.12 = (f32[512,128]{1,0:T(8,128)S(1)}, f32[512,128]{1,0:T(8,128)S(1)}, u32[]{:S(2)}, u32[]{:S(2)}) collective-permute-start(f32[512,128]{1,0:T(8,128)S(1)} %pad_maximum_fusion), channel_id=1, source_target_pairs={{0,1},{1,0},{2,3},{3,2},{4,5},{5,4},{6,7},{7,6},{8,9},{9,8},{10,11... | collective-permute-start | bytes 786440 | tf_op jit(solution)/shard_map/ppermute | solution.py:196
  55.5 0.5 collective-permute-done.1.refs_1_
  55.9 1.2 %collective-permute-done.10 = f32[256,128]{1,0:T(8,128)S(1)} collective-permute-done((f32[256,128]{1,0:T(8,128)S(1)}, f32[256,128]{1,0:T(8,128)S(1)}, u32[]{:S(2)}, u32[]{:S(2)}) %collective-permute-start.10) | collective-permute-done | bytes 131104 | tf_op jit(solution)/shard_map/ppermute | solution.py:196
  57.1 2.6 %shard_map.102 = (f32[128,1024]{1,0:T(8,128)S(1)}, f32[128,1024]{1,0:T(8,128)S(1)}, f32[256,128]{1,0:T(8,128)S(1)}) custom-call(s32[1]{0:T(128)} %bitcast.rep_ref, bf16[512,1024]{1,0:T(8,128)(2,1)S(1)} %collective-permute-done.refs_0_, bf16[512,128]{1,0:T(8,128)(2,1)S(1)} %collective-permute-done.1.refs_1_, f32[7,1024]{1,0:T(8,128)S(1)} %get-tuple-element.89.refs_2_.refs_1_, ...), custom_call_target="tpu_custom_call" | custom-call | flops 1 | bytes 1 | tf_op jit(solution)/shard_map/pallas_call | solution.py:159
  59.8 2.6 %shard_map.103 = (f32[128,1024]{1,0:T(8,128)S(1)}, f32[128,1024]{1,0:T(8,128)S(1)}, f32[256,128]{1,0:T(8,128)S(1)}) custom-call(s32[1]{0:T(128)} %bitcast.rep_ref, bf16[512,1024]{1,0:T(8,128)(2,1)S(1)} %collective-permute-done.refs_0_, bf16[512,128]{1,0:T(8,128)(2,1)S(1)} %collective-permute-done.1.refs_1_, f32[7,1024]{1,0:T(8,128)S(1)} %get-tuple-element.89.refs_2_.refs_1_, ...), custom_call_target="tpu_custom_call" | custom-call | flops 10000000000 | bytes 1 | tf_op jit(solution)/shard_map/pallas_call | solution.py:159
  62.4 0.1 collective-permute-start.15
  62.5 2.9 %collective-permute-start.13 = (f32[256,128]{1,0:T(8,128)S(1)}, f32[256,128]{1,0:T(8,128)S(1)}, u32[]{:S(2)}, u32[]{:S(2)}) collective-permute-start(f32[256,128]{1,0:T(8,128)S(1)} %get-tuple-element.77), channel_id=1, source_target_pairs={{0,5},{1,4},{2,7},{3,6},{4,1},{5,0},{6,3},{7,2},{8,13},{9,12},{10,... | collective-permute-start | bytes 393224 | tf_op jit(solution)/shard_map/ppermute | solution.py:196
  65.4 4.6 %collective-permute-start.11 = (f32[128,1024]{1,0:T(8,128)S(1)}, f32[128,1024]{1,0:T(8,128)S(1)}, u32[]{:S(2)}, u32[]{:S(2)}) collective-permute-start(f32[128,1024]{1,0:T(8,128)S(1)} %get-tuple-element.73), channel_id=1, source_target_pairs={{0,2},{1,3},{2,0},{3,1},{4,6},{5,7},{6,4},{7,5},{8,10},{9,11},{10,... | collective-permute-start | bytes 1572872 | tf_op jit(solution)/shard_map/ppermute | solution.py:196
  70.0 0.1 collective-permute-start.14
  70.1 0.0 collective-permute-done.15
  70.2 4.4 %collective-permute-done.14 = f32[256,128]{1,0:T(8,128)S(1)} collective-permute-done((f32[256,128]{1,0:T(8,128)S(1)}, f32[256,128]{1,0:T(8,128)S(1)}, u32[]{:S(2)}, u32[]{:S(2)}) %collective-permute-start.14) | collective-permute-done | bytes 131104 | tf_op jit(solution)/shard_map/ppermute | solution.py:196
  74.5 0.7 fusion.4
  75.2 0.1 add_bitcast_fusion
  75.3 1.0 %copy.12 = f32[1024,128]{1,0:T(8,128)} copy(f32[1024,128]{0,1:T(8,128)S(1)} %add_bitcast_fusion) | data formatting | bytes 1048576
  (22 shorter events, 0.1 us)
Async XLA Ops:
  0.6 16.7 %copy-start = (bf16[1024,128]{1,0:T(8,128)(2,1)S(1)}, bf16[1024,128]{1,0:T(8,128)(2,1)}, u32[]{:S(2)}) copy-start(bf16[1024,128]{1,0:T(8,128)(2,1)} %refs_6_.7) | copy-start | bytes 786436
  0.6 16.7 %copy-start.1 = (bf16[512,1024]{1,0:T(8,128)(2,1)S(1)}, bf16[512,1024]{1,0:T(8,128)(2,1)}, u32[]{:S(2)}) copy-start(bf16[512,1024]{1,0:T(8,128)(2,1)} %refs_0_.1) | copy-start | bytes 3145732
  0.7 21.0 %collective-permute-start.6 = (bf16[1024,1024]{1,0:T(8,128)(2,1)}, bf16[1024,1024]{1,0:T(8,128)(2,1)}, u32[]{:S(2)}, u32[]{:S(2)}) collective-permute-start(bf16[1024,1024]{1,0:T(8,128)(2,1)} %tq_ref.1), channel_id=1, source_target_pairs={{0,2},{1,3},{2,0},{3,1},{4,6},{5,7},{6,4},{7,5},{8,10},{9,11},{10,... | collective-permute-start | bytes 6291464 | tf_op jit(solution)/shard_map/ppermute | solution.py:196
  4.0 17.6 %collective-permute-start.7 = (bf16[1024,128]{1,0:T(8,128)(2,1)}, bf16[1024,128]{1,0:T(8,128)(2,1)S(1)}, u32[]{:S(2)}, u32[]{:S(2)}) collective-permute-start(bf16[1024,128]{1,0:T(8,128)(2,1)} %refs_6_.7), channel_id=1, source_target_pairs={{0,2},{1,3},{2,0},{3,1},{4,6},{5,7},{6,4},{7,5},{8,10},{9,11},{10,... | collective-permute-start | bytes 786440 | tf_op jit(solution)/shard_map/ppermute | solution.py:196
  4.1 15.6 %copy-start.3 = (bf16[512,128]{1,0:T(8,128)(2,1)S(1)}, bf16[512,128]{1,0:T(8,128)(2,1)}, u32[]{:S(2)}) copy-start(bf16[512,128]{1,0:T(8,128)(2,1)} %refs_1_.1) | copy-start | bytes 393220
  6.0 22.6 %collective-permute-start.4 = (bf16[256,1152]{1,0:T(8,128)(2,1)}, bf16[256,1152]{1,0:T(8,128)(2,1)S(1)}, u32[]{:S(2)}, u32[]{:S(2)}) collective-permute-start(bf16[256,1152]{1,0:T(8,128)(2,1)} %shard_map.95), channel_id=1, source_target_pairs={{0,253},{1,252},{2,255},{3,254},{4,9},{5,8},{6,11},{7,10},{8,5},{9... | collective-permute-start | bytes 1769480 | tf_op jit(solution)/shard_map/ppermute | solution.py:196
  16.6 3.1 %collective-permute-start.5 = (f32[8,1024]{1,0:T(8,128)S(1)}, f32[8,1024]{1,0:T(8,128)S(1)}, u32[]{:S(2)}, u32[]{:S(2)}) collective-permute-start(f32[8,1024]{1,0:T(8,128)S(1)} %pad_maximum_fusion.1), channel_id=1, source_target_pairs={{0,2},{1,3},{2,0},{3,1},{4,6},{5,7},{6,4},{7,5},{8,10},{9,11},{10,... | collective-permute-start | bytes 98312 | tf_op jit(solution)/shard_map/ppermute | solution.py:196
  17.4 20.5 %collective-permute-start.2 = (bf16[512,1024]{1,0:T(8,128)(2,1)S(1)}, bf16[512,1024]{1,0:T(8,128)(2,1)S(1)}, u32[]{:S(2)}, u32[]{:S(2)}) collective-permute-start(bf16[512,1024]{1,0:T(8,128)(2,1)S(1)} %copy-done.1), channel_id=1, source_target_pairs={{0,250},{1,251},{2,8},{3,9},{4,254},{5,255},{6,12},{7,13},{8,2},{9... | collective-permute-start | bytes 3145736 | tf_op jit(solution)/shard_map/ppermute | solution.py:196
  17.4 1.6 %copy-start.2 = (bf16[1024,1024]{1,0:T(8,128)(2,1)S(1)}, bf16[1024,1024]{1,0:T(8,128)(2,1)}, u32[]{:S(2)}) copy-start(bf16[1024,1024]{1,0:T(8,128)(2,1)} %tq_ref.1) | copy-start | bytes 6291460
  19.7 18.2 %collective-permute-start.3 = (bf16[512,128]{1,0:T(8,128)(2,1)S(1)}, bf16[512,128]{1,0:T(8,128)(2,1)S(1)}, u32[]{:S(2)}, u32[]{:S(2)}) collective-permute-start(bf16[512,128]{1,0:T(8,128)(2,1)S(1)} %copy-done.3), channel_id=1, source_target_pairs={{0,250},{1,251},{2,8},{3,9},{4,254},{5,255},{6,12},{7,13},{8,2},{9... | collective-permute-start | bytes 393224 | tf_op jit(solution)/shard_map/ppermute | solution.py:196
  21.5 34.4 %collective-permute-start = (bf16[512,1024]{1,0:T(8,128)(2,1)S(1)}, bf16[512,1024]{1,0:T(8,128)(2,1)S(1)}, u32[]{:S(2)}, u32[]{:S(2)}) collective-permute-start(bf16[512,1024]{1,0:T(8,128)(2,1)S(1)} %copy-done.1), channel_id=1, source_target_pairs={{0,5},{1,4},{2,7},{3,6},{4,1},{5,0},{6,3},{7,2},{8,13},{9,12},{10,... | collective-permute-start | bytes 3145736 | tf_op jit(solution)/shard_map/ppermute | solution.py:196
  28.6 13.9 %collective-permute-start.8 = (bf16[256,1152]{1,0:T(8,128)(2,1)S(1)}, bf16[256,1152]{1,0:T(8,128)(2,1)S(1)}, u32[]{:S(2)}, u32[]{:S(2)}) collective-permute-start(bf16[256,1152]{1,0:T(8,128)(2,1)S(1)} %collective-permute-done.4.refs_0_), channel_id=1, source_target_pairs={{0,1},{1,0},{2,3},{3,2},{4,5},{5,4},{6,7},{7,6},{8,9},{9,8},{10,11... | collective-permute-start | bytes 1769480 | tf_op jit(solution)/shard_map/ppermute | solution.py:196
  31.6 11.0 %collective-permute-start.9 = (f32[256,128]{1,0:T(8,128)S(1)}, f32[256,128]{1,0:T(8,128)S(1)}, u32[]{:S(2)}, u32[]{:S(2)}) collective-permute-start(f32[256,128]{1,0:T(8,128)S(1)} %get-tuple-element.54), channel_id=1, source_target_pairs={{0,253},{1,252},{2,255},{3,254},{4,9},{5,8},{6,11},{7,10},{8,5},{9... | collective-permute-start | bytes 393224 | tf_op jit(solution)/shard_map/ppermute | solution.py:196
  37.9 18.1 %collective-permute-start.1 = (bf16[512,128]{1,0:T(8,128)(2,1)S(1)}, bf16[512,128]{1,0:T(8,128)(2,1)S(1)}, u32[]{:S(2)}, u32[]{:S(2)}) collective-permute-start(bf16[512,128]{1,0:T(8,128)(2,1)S(1)} %copy-done.3), channel_id=1, source_target_pairs={{0,5},{1,4},{2,7},{3,6},{4,1},{5,0},{6,3},{7,2},{8,13},{9,12},{10,... | collective-permute-start | bytes 393224 | tf_op jit(solution)/shard_map/ppermute | solution.py:196
  47.3 9.8 %collective-permute-start.10 = (f32[256,128]{1,0:T(8,128)S(1)}, f32[256,128]{1,0:T(8,128)S(1)}, u32[]{:S(2)}, u32[]{:S(2)}) collective-permute-start(f32[256,128]{1,0:T(8,128)S(1)} %get-tuple-element.65), channel_id=1, source_target_pairs={{0,252},{1,253},{2,254},{3,255},{4,8},{5,9},{6,10},{7,11},{8,4},{9... | collective-permute-start | bytes 393224 | tf_op jit(solution)/shard_map/ppermute | solution.py:196
  54.1 16.0 %collective-permute-start.12 = (f32[512,128]{1,0:T(8,128)S(1)}, f32[512,128]{1,0:T(8,128)S(1)}, u32[]{:S(2)}, u32[]{:S(2)}) collective-permute-start(f32[512,128]{1,0:T(8,128)S(1)} %pad_maximum_fusion), channel_id=1, source_target_pairs={{0,1},{1,0},{2,3},{3,2},{4,5},{5,4},{6,7},{7,6},{8,9},{9,8},{10,11... | collective-permute-start | bytes 786440 | tf_op jit(solution)/shard_map/ppermute | solution.py:196
  62.4 7.7 %collective-permute-start.15 = (f32[256,128]{1,0:T(8,128)S(1)}, f32[256,128]{1,0:T(8,128)S(1)}, u32[]{:S(2)}, u32[]{:S(2)}) collective-permute-start(f32[256,128]{1,0:T(8,128)S(1)} %get-tuple-element.79), channel_id=1, source_target_pairs={{0,4},{1,5},{2,6},{3,7},{4,0},{5,1},{6,2},{7,3},{8,12},{9,13},{10,... | collective-permute-start | bytes 393224 | tf_op jit(solution)/shard_map/ppermute | solution.py:196
  62.5 7.6 %collective-permute-start.13 = (f32[256,128]{1,0:T(8,128)S(1)}, f32[256,128]{1,0:T(8,128)S(1)}, u32[]{:S(2)}, u32[]{:S(2)}) collective-permute-start(f32[256,128]{1,0:T(8,128)S(1)} %get-tuple-element.77), channel_id=1, source_target_pairs={{0,5},{1,4},{2,7},{3,6},{4,1},{5,0},{6,3},{7,2},{8,13},{9,12},{10,... | collective-permute-start | bytes 393224 | tf_op jit(solution)/shard_map/ppermute | solution.py:196
  65.4 9.8 %collective-permute-start.11 = (f32[128,1024]{1,0:T(8,128)S(1)}, f32[128,1024]{1,0:T(8,128)S(1)}, u32[]{:S(2)}, u32[]{:S(2)}) collective-permute-start(f32[128,1024]{1,0:T(8,128)S(1)} %get-tuple-element.73), channel_id=1, source_target_pairs={{0,2},{1,3},{2,0},{3,1},{4,6},{5,7},{6,4},{7,5},{8,10},{9,11},{10,... | collective-permute-start | bytes 1572872 | tf_op jit(solution)/shard_map/ppermute | solution.py:196
  70.0 4.5 %collective-permute-start.14 = (f32[256,128]{1,0:T(8,128)S(1)}, f32[256,128]{1,0:T(8,128)S(1)}, u32[]{:S(2)}, u32[]{:S(2)}) collective-permute-start(f32[256,128]{1,0:T(8,128)S(1)} %slice_add_fusion), channel_id=1, source_target_pairs={{0,250},{1,251},{2,8},{3,9},{4,254},{5,255},{6,12},{7,13},{8,2},{9... | collective-permute-start | bytes 393224 | tf_op jit(solution)/shard_map/ppermute | solution.py:196

commit v3 on v2

--- a/solution.py
+++ b/solution.py
@@ -66,28 +66,37 @@
     return p, y ^ 1, c
 
 
-def gather_kernel(rep_ref, teacher_ref, student_ref, out_ref, sems):
-    rows = out_ref.shape[0]
-    part = pl.ds(pl.multiple_of(rep_ref[0] * rows, rows), rows)
+def gather_kernel(parts, rep_ref, teacher_ref, student_ref, *refs):
+    *out_refs, sems = refs
+    width = teacher_ref.shape[1]
+    half = teacher_ref.shape[0] // 2
     copies = []
-    for source, first in ((teacher_ref, 0), (student_ref, teacher_ref.shape[1])):
-        target = out_ref.at[:, pl.ds(first, source.shape[1])]
-        copies.append(pltpu.make_async_copy(source.at[part, :], target, sems.at[len(copies)]))
+    for out_ref, (other, skipped) in zip(out_refs, parts, strict=True):
+        rows = out_ref.shape[0]
+        for first in range(0, rows, half):
+            swap = (other or first > 0) != 0
+            start = pl.multiple_of((1 - rep_ref[0] if swap else rep_ref[0]) * half, half) + skipped
+            count = min(rows, half)
+            for source, column in ((teacher_ref, 0), (student_ref, width)):
+                target = out_ref.at[pl.ds(first, count), pl.ds(column, source.shape[1])]
+                copies.append(
+                    pltpu.make_async_copy(source.at[pl.ds(start, count), :], target, sems.at[len(copies)])
+                )
     for copy in copies:
         copy.start()
     for copy in copies:
         copy.wait()
 
 
-def gather(rep, teacher, student):
-    rows, width = teacher.shape[0] // 2, teacher.shape[1] + student.shape[1]
+def gather(parts, rep, teacher, student):
+    width = teacher.shape[1] + student.shape[1]
     whole = pl.BlockSpec(memory_space=pl.ANY)
     return pl.pallas_call(
-        gather_kernel,
-        out_shape=jax.ShapeDtypeStruct((rows, width), teacher.dtype),
+        functools.partial(gather_kernel, [part[:2] for part in parts]),
+        out_shape=[jax.ShapeDtypeStruct((part[2], width), teacher.dtype) for part in parts],
         in_specs=[pl.BlockSpec(memory_space=pltpu.SMEM), whole, whole],
-        out_specs=pl.BlockSpec(memory_space=pltpu.VMEM),
-        scratch_shapes=[pltpu.SemaphoreType.DMA((2,))],
+        out_specs=[pl.BlockSpec(memory_space=pltpu.VMEM)] * len(parts),
+        scratch_shapes=[pltpu.SemaphoreType.DMA((4 * len(parts),))],
         compiler_params=pltpu.CompilerParams(vmem_limit_bytes=56 << 20),
         cost_estimate=pl.CostEstimate(flops=1, bytes_accessed=1, transcendentals=0),
     )(rep, teacher, student)
@@ -112,22 +121,14 @@
     )(tq, sq)
 
 
-def visit_kernel(parts, rows, first, scales, rep_ref, *refs):
+def visit_kernel(pieces, rows, first, scales, *refs):
     groups = len(rows)
     term_ref = refs[-1]
-    if parts is None:
-        width = refs[0].shape[1] - term_ref.shape[1]
-        teacher, student = refs[0][:, :width], refs[0][:, width:]
-        refs = refs[1:]
-    else:
-        half = refs[0].shape[0] // 2
-        rep = rep_ref[0]
-        picks = [pl.ds(pl.multiple_of((1 - rep if part else rep) * half, half), half) for part in parts]
-        teacher, student = (
-            jnp.concatenate([ref[pick, :] for pick in picks]) if len(picks) > 1 else ref[picks[0], :]
-            for ref in refs[:2]
-        )
-        refs = refs[2:]
+    piece = [ref[...] for ref in refs[:pieces]]
+    piece = piece[0] if pieces == 1 else jnp.concatenate(piece)
+    refs = refs[pieces:]
+    width = piece.shape[1] - term_ref.shape[1]
+    teacher, student = piece[:, :width], piece[:, width:]
     term = None
     for group, row in enumerate(rows):
         zt_ref, zs_ref, tqt_ref, sqt_ref, sq_ref = refs[group * 5 : group * 5 + 5]
@@ -148,23 +149,23 @@
     term_ref[...] = term
 
 
-def visit(rep, piece, parts, rows, groups, scales, totals, cost=1):
+def visit(pieces, rows, groups, scales, totals, cost=1):
     width, requests = groups[0][3].shape
     vmem = pl.BlockSpec(memory_space=pltpu.VMEM)
-    items = piece[0].shape[0] if parts is None else piece[0].shape[0] // 2 * len(parts)
-    operands = [*piece]
+    items = sum(piece.shape[0] for piece in pieces)
+    operands = [*pieces]
     for group in groups:
         operands.extend(group)
     operands.extend(totals)
     *totals, term = pl.pallas_call(
-        functools.partial(visit_kernel, parts, rows, not totals, scales),
+        functools.partial(visit_kernel, len(pieces), rows, not totals, scales),
         out_shape=tuple([jax.ShapeDtypeStruct((width, requests), jnp.float32)] * len(groups))
         + (jax.ShapeDtypeStruct((items, width), jnp.float32),),
-        in_specs=[pl.BlockSpec(memory_space=pltpu.SMEM)] + [vmem] * len(operands),
+        in_specs=[vmem] * len(operands),
         out_specs=(vmem,) * (len(groups) + 1),
         compiler_params=pltpu.CompilerParams(vmem_limit_bytes=24 << 20),
         cost_estimate=pl.CostEstimate(flops=cost, bytes_accessed=1, transcendentals=0),
-    )(rep, *operands)
+    )(*operands)
     return totals, term
 
 
@@ -183,6 +184,7 @@
     blocks = block_mask.shape[0]
     span = teacher_items.shape[0]
     half = span // 2
+    quarter = half // 2
     teacher_scale = score_gain / math.sqrt(teacher_queries.shape[1])
     student_scale = score_gain / math.sqrt(student_queries.shape[1])
     scales = (teacher_scale / logit_cap, student_scale / logit_cap)
@@ -199,10 +201,9 @@
         return lax.optimization_barrier(blocks)
 
     where = jnp.reshape(rep, (1,)).astype(jnp.int32)
-    diag_half = send(gather(where, teacher_items, student_items), diag)
-    own = (teacher_items, student_items)
-    far_span = [send(block, far) for block in own]
-    across = [send(block, cross) for block in own]
+    (half_mine,) = gather([(0, 0, half)], where, teacher_items, student_items)
+    diag_half = send(half_mine, diag)
+    own, tail = gather([(0, 0, span), (1, quarter, quarter)], where, teacher_items, student_items)
     other_tq = send(teacher_queries, core)
     other_sq = send(student_queries, core)
 
@@ -225,28 +226,41 @@
     mine = (zt_all, zs_all, *turn(teacher_queries, student_queries), student_queries)
     other = (other_z[:4], other_z[4:], *turn(other_tq, other_sq), other_sq)
     both = (mine, other)
-    q, own_term = visit(where, own, (0, 1), (0, 1), both, scales, [])
-
-    diag_half, q, own_term = stage(diag_half, q, own_term)
+    half_mine, own_too, _ = stage(half_mine, own, other[2])
+    cross_half = send(half_mine, cross)
+    far_span = send(own_too, far)
+    q, own_term = visit([own], (0, 1), both, scales, [])
+
+    diag_half, tail, q, own_term = stage(diag_half, tail, q, own_term)
     next_half = send(diag_half, pair)
-    q, diag_term = visit(where, [diag_half], None, (2, 3), both, scales, q, cost=long_cost)
+    cross_tail = send(tail, cross)
+    q, diag_term = visit([diag_half], (2, 3), both, scales, q, cost=long_cost)
     diag_back = send(diag_term, diag)
-
-    far_span, next_half, q, own_term, diag_back = stage(far_span, next_half, q, own_term, diag_back)
-    q[:1], far_term = visit(where, far_span, (0, 1), (3,), both[:1], scales, q[:1])
+    far_span, q, own_term = stage(far_span, q, own_term)
+    q[:1], far_term = visit([far_span], (3,), both[:1], scales, q[:1], cost=long_cost)
     pair_back = send(jnp.concatenate([own_term[half:], far_term[half:]]), pair)
-    q, next_term = visit(where, [next_half], None, (2, 3), both, scales, q)
+
+    cross_half, next_half, q, own_term, far_term, diag_back = stage(
+        cross_half, next_half, q, own_term, far_term, diag_back
+    )
+    cross_head = send(cross_half[:quarter], pair)
+    q, next_term = visit([next_half], (2, 3), both, scales, q, cost=long_cost)
     next_back = send(next_term, diag_two)
-
-    across, q, own_term, far_term, next_back = stage(across, q, own_term, far_term, next_back)
-    q, first_term = visit(where, across, (1,), (1, 2), both, scales, q)
-    cross_back = send(first_term, cross)
+    q, cross_term = visit([cross_half], (1, 2), both, scales, q, cost=long_cost)
+    cross_back = send(cross_term, cross)
     far_back = send(far_term[:half] + pair_back[half:], far)
-    q, last_term = visit(where, across, (0,), (1, 2), both, scales, q, cost=long_cost)
-    q = q[0] + send(q[1], core)
-    last_back = send(last_term, two)
-    total = own_term[:half] + pair_back[:half] + diag_back + next_back
-    return q.T, total + cross_back + far_back + last_back
+
+    cross_head, cross_tail, q, own_term, pair_back = stage(
+        cross_head, cross_tail, q, own_term, pair_back
+    )
+    rest = [cross_head, cross_tail]
+    q[1:], other_term = visit(rest, (2,), both[1:], scales, q[1:], cost=long_cost)
+    q_back = send(q[1], core)
+    q[:1], last_term = visit(rest, (1,), both[:1], scales, q[:1], cost=long_cost)
+    last_back = send((last_term + other_term).astype(jnp.bfloat16), two)
+    total = own_term[:half] + pair_back[:half] + diag_back + next_back + cross_back + far_back
+    q_out, total = stage((q[0] + q_back).T, total)
+    return q_out, total + last_back.astype(jnp.float32)
 
 
 def solution(mesh):

time: 77 us -> 68.8 us (0.89)
  starting transfers between devices: 37.1 us -> 30.8 us
  Pallas kernels: 22.3 us -> 24.9 us
  waiting for transfers between devices: 10.6 us -> 8.01 us
  local copies, waits for them, and re-layouts: 2.9 us -> 1.35 us
    ppermute x16, starting transfers between devices: 37.1 us -> 30.8 us  [send(): return lax.ppermute(block, AXES, edges(n_items, move))]
    ppermute x16, waiting for transfers between devices: 10.6 us -> 8.01 us  [send(): return lax.ppermute(block, AXES, edges(n_items, move))]
    pallas_call x7 -> x9, Pallas kernels: 19.3 us -> 21.8 us  [the longest x7 17.4 us: visit(): pl.pallas_call(functools.partial(visit_kernel, len(pieces), rows, not tot...]
    unnamed x9 -> x11, local copies, waits for them, and re-layouts: 2.59 us -> 1.02 us
  transfers between devices with their start and end apart: 16 -> 16, of which waited for: 4 -> 5; matrix products, arithmetic and copies ran while one was open for 4% -> 5% of each run, Pallas kernels for 29% -> 36%
where the time goes in v3:
time: 68.8 us; the launch traced here: 68.5 us
  starting transfers between devices  30.8 us (45%)
  Pallas kernels  24.9 us (36%)
  waiting for transfers between devices  8.01 us (12%)
  other arithmetic  2.5 us (4%)
  local copies, waits for them, and re-layouts  1.35 us (2%)
  between operations  1.02 us (1%)
    ppermute x16, starting transfers between devices, send(): return lax.ppermute(block, AXES, edges(n_items, move))  30.8 us
    pallas_call x7, Pallas kernels, visit(): pl.pallas_call(functools.partial(visit_kernel, len(pieces), rows, not tot...  17.4 us
    ppermute x16, waiting for transfers between devices, send(): return lax.ppermute(block, AXES, edges(n_items, move))  8.01 us
    pallas_call x2, Pallas kernels, gather(): pl.pallas_call(functools.partial(gather_kernel, [part[:2] for part in par...  4.37 us
    pallas_call x2, Pallas kernels, turn(): pl.pallas_call(turn_kernel, out_shape=tuple((pltpu.VMEM(block.shape[::-1]...  3.12 us
  transfers between devices with their start and end apart: 16, of which 5 were waited for; matrix products, arithmetic and copies ran while one was open for 5% of the time, Pallas kernels for 36%

profile of v3, /device:TPU:1, one launch (start us, length us, event | category | flops | bytes accessed | tf_op | source)
XLA Modules:
  0.0 68.5 jit_solution(9631418501192646858)
XLA Ops:
  0.6 3.3 %collective-permute-start = (bf16[1024,1024]{1,0:T(8,128)(2,1)}, bf16[1024,1024]{1,0:T(8,128)(2,1)}, u32[]{:S(2)}, u32[]{:S(2)}) collective-permute-start(bf16[1024,1024]{1,0:T(8,128)(2,1)} %tq_ref.1), channel_id=1, source_target_pairs={{0,2},{1,3},{2,0},{3,1},{4,6},{5,7},{6,4},{7,5},{8,10},{9,11},{10,... | collective-permute-start | bytes 6291464 | tf_op jit(solution)/shard_map/ppermute | solution.py:198
  4.0 0.1 collective-permute-start.1
  4.1 1.9 %shard_map.95 = bf16[256,1152]{1,0:T(8,128)(2,1)} custom-call(s32[1]{0:T(128)} %bitcast.rep_ref, bf16[512,1024]{1,0:T(8,128)(2,1)} %teacher_ref.3, bf16[512,128]{1,0:T(8,128)(2,1)} %student_ref.3), custom_call_target="tpu_custom_call" | custom-call | flops 1 | bytes 1 | tf_op jit(solution)/shard_map/pallas_call | solution.py:94
  6.0 0.0 copy-start
  6.0 0.0 copy-start.2
  6.0 8.6 %collective-permute-start.3 = (bf16[256,1152]{1,0:T(8,128)(2,1)}, bf16[256,1152]{1,0:T(8,128)(2,1)S(1)}, u32[]{:S(2)}, u32[]{:S(2)}) collective-permute-start(bf16[256,1152]{1,0:T(8,128)(2,1)} %shard_map.95), channel_id=1, source_target_pairs={{0,253},{1,252},{2,255},{3,254},{4,9},{5,8},{6,11},{7,10},{8,5},{9... | collective-permute-start | bytes 1769480 | tf_op jit(solution)/shard_map/ppermute | solution.py:198
  14.6 0.1 stack.27
  14.6 0.1 iota_compare_fusion.1
  14.7 0.7 %broadcast_compare_fusion = pred[16,7]{0,1:T(8,128)(4,1)S(1)} fusion(s32[16,7]{0,1:T(8,128)} %param.12), kind=kLoop, calls=%fused_computation.16 | loop fusion | flops 112 | bytes 560 | tf_op jit(solution)/shard_map/ne | solution.py:220
  15.4 0.1 and_reduce_fusion
  15.5 0.1 broadcast_in_dim.31
  15.6 0.1 reshape.101
  15.7 0.8 %select_reduce_fusion = (f32[1024]{0:T(1024)S(1)}, f32[1024]{0:T(1024)S(1)}) fusion(f32[4,1024]{1,0:T(4,128)} %param.15, s32[1024]{0:T(1024)} %param.13, f32[4,1024]{1,0:T(4,128)} %param.14), kind=kLoop, calls=%fused_computation.9 | loop fusion | flops 18432 | bytes 45056 | tf_op jit(solution)/shard_map/reduce_sum | solution.py:214
  16.6 0.8 %collective-permute-start.4 = (f32[8,1024]{1,0:T(8,128)S(1)}, f32[8,1024]{1,0:T(8,128)S(1)}, u32[]{:S(2)}, u32[]{:S(2)}) collective-permute-start(f32[8,1024]{1,0:T(8,128)S(1)} %pad_maximum_fusion.1), channel_id=1, source_target_pairs={{0,2},{1,3},{2,0},{3,1},{4,6},{5,7},{6,4},{7,5},{8,10},{9,11},{10,... | collective-permute-start | bytes 98312 | tf_op jit(solution)/shard_map/ppermute | solution.py:198
  17.3 2.5 %shard_map.96 = (bf16[512,1152]{1,0:T(8,128)(2,1)}, bf16[128,1152]{1,0:T(8,128)(2,1)}) custom-call(s32[1]{0:T(128)} %bitcast.rep_ref, bf16[512,1024]{1,0:T(8,128)(2,1)} %teacher_ref.3, bf16[512,128]{1,0:T(8,128)(2,1)} %student_ref.3), custom_call_target="tpu_custom_call" | custom-call | flops 1 | bytes 1 | tf_op jit(solution)/shard_map/pallas_call | solution.py:94
  19.8 0.0 collective-permute-done.1.sq_ref.refs_10_.refs_6_
  19.9 2.4 %shard_map.97 = (bf16[1024,1024]{1,0:T(8,128)(2,1)S(1)}, bf16[128,1024]{1,0:T(8,128)(2,1)S(1)}) custom-call(bf16[1024,1024]{1,0:T(8,128)(2,1)} %collective-permute-done.tq_ref, bf16[1024,128]{1,0:T(8,128)(2,1)S(1)} %collective-permute-done.1.sq_ref.refs_10_.refs_6_), custom_call_target="tpu_custom_call" | custom-call | flops 1 | bytes 1 | tf_op jit(solution)/shard_map/pallas_call | solution.py:114
  22.3 0.1 collective-permute-start.6
  22.4 0.7 %shard_map.98 = (bf16[1024,1024]{1,0:T(8,128)(2,1)S(1)}, bf16[128,1024]{1,0:T(8,128)(2,1)S(1)}) custom-call(bf16[1024,1024]{1,0:T(8,128)(2,1)S(1)} %copy-done, bf16[1024,128]{1,0:T(8,128)(2,1)S(1)} %copy-done.2), custom_call_target="tpu_custom_call" | custom-call | flops 1 | bytes 1 | tf_op jit(solution)/shard_map/pallas_call | solution.py:114
  23.1 0.0 collective-permute-done.4
  23.2 0.1 collective-permute-start.2
  23.3 4.7 %shard_map.99 = (f32[128,1024]{1,0:T(8,128)S(1)}, f32[128,1024]{1,0:T(8,128)S(1)}, f32[512,128]{1,0:T(8,128)S(1)}) custom-call(bf16[512,1152]{1,0:T(8,128)(2,1)S(1)} %copy-done.1, f32[7,1024]{1,0:T(8,128)S(1)} %get-tuple-element.111.refs_1_.refs_2_, f32[7,1024]{1,0:T(8,128)S(1)} %get-tuple-element.110.refs_2_.refs_3_, ...), custom_call_target="tpu_custom_call" | custom-call | flops 1 | bytes 1 | tf_op jit(solution)/shard_map/pallas_call | solution.py:160
  28.0 0.2 collective-permute-done.3.refs_0_
  28.1 0.0 collective-permute-start.5
  28.1 2.6 %shard_map.100 = (f32[128,1024]{1,0:T(8,128)S(1)}, f32[128,1024]{1,0:T(8,128)S(1)}, f32[256,128]{1,0:T(8,128)S(1)}) custom-call(bf16[256,1152]{1,0:T(8,128)(2,1)S(1)} %collective-permute-done.3.refs_0_, f32[7,1024]{1,0:T(8,128)S(1)} %get-tuple-element.111.refs_1_.refs_2_, f32[7,1024]{1,0:T(8,128)S(1)} %get-tuple-element.110.refs_2_.refs_3_, ...), custom_call_target="tpu_custom_call" | custom-call | flops 10000000000 | bytes 1 | tf_op jit(solution)/shard_map/pallas_call | solution.py:160
  30.8 7.3 %collective-permute-start.7 = (f32[256,128]{1,0:T(8,128)S(1)}, f32[256,128]{1,0:T(8,128)S(1)}, u32[]{:S(2)}, u32[]{:S(2)}) collective-permute-start(f32[256,128]{1,0:T(8,128)S(1)} %get-tuple-element.75), channel_id=1, source_target_pairs={{0,253},{1,252},{2,255},{3,254},{4,9},{5,8},{6,11},{7,10},{8,5},{9... | collective-permute-start | bytes 393224 | tf_op jit(solution)/shard_map/ppermute | solution.py:198
  38.0 0.0 collective-permute-start.9
  38.0 1.7 %collective-permute-done.6.refs_0_ = bf16[512,1152]{1,0:T(8,128)(2,1)S(1)} collective-permute-done((bf16[512,1152]{1,0:T(8,128)(2,1)S(1)}, bf16[512,1152]{1,0:T(8,128)(2,1)S(1)}, u32[]{:S(2)}, u32[]{:S(2)}) %collective-permute-start.6) | collective-permute-done | bytes 1179680 | tf_op jit(solution)/shard_map/ppermute | solution.py:198
  39.7 2.2 %shard_map.101 = (f32[128,1024]{1,0:T(8,128)S(1)}, f32[512,128]{1,0:T(8,128)S(1)}) custom-call(bf16[512,1152]{1,0:T(8,128)(2,1)S(1)} %collective-permute-done.6.refs_0_, f32[7,1024]{1,0:T(8,128)S(1)} %get-tuple-element.111.refs_1_.refs_2_, f32[7,1024]{1,0:T(8,128)S(1)} %get-tuple-element.110.refs_2_.refs_3_, ...), custom_call_target="tpu_custom_call" | custom-call | flops 10000000000 | bytes 1 | tf_op jit(solution)/shard_map/pallas_call | solution.py:160
  41.9 0.1 collective-permute-start.10
  42.0 2.0 %collective-permute-done.7 = f32[256,128]{1,0:T(8,128)S(1)} collective-permute-done((f32[256,128]{1,0:T(8,128)S(1)}, f32[256,128]{1,0:T(8,128)S(1)}, u32[]{:S(2)}, u32[]{:S(2)}) %collective-permute-start.7) | collective-permute-done | bytes 131104 | tf_op jit(solution)/shard_map/ppermute | solution.py:198
  44.1 0.0 collective-permute-done.2.refs_0_
  44.1 0.1 collective-permute-start.8
  44.2 2.6 %shard_map.102 = (f32[128,1024]{1,0:T(8,128)S(1)}, f32[128,1024]{1,0:T(8,128)S(1)}, f32[256,128]{1,0:T(8,128)S(1)}) custom-call(bf16[256,1152]{1,0:T(8,128)(2,1)S(1)} %collective-permute-done.5.refs_0_, f32[7,1024]{1,0:T(8,128)S(1)} %get-tuple-element.111.refs_1_.refs_2_, f32[7,1024]{1,0:T(8,128)S(1)} %get-tuple-element.110.refs_2_.refs_3_, ...), custom_call_target="tpu_custom_call" | custom-call | flops 10000000000 | bytes 1 | tf_op jit(solution)/shard_map/pallas_call | solution.py:160
  46.9 2.6 %shard_map.103 = (f32[128,1024]{1,0:T(8,128)S(1)}, f32[128,1024]{1,0:T(8,128)S(1)}, f32[256,128]{1,0:T(8,128)S(1)}) custom-call(bf16[256,1152]{1,0:T(8,128)(2,1)S(1)} %collective-permute-done.2.refs_0_, f32[7,1024]{1,0:T(8,128)S(1)} %get-tuple-element.111.refs_1_.refs_2_, f32[7,1024]{1,0:T(8,128)S(1)} %get-tuple-element.110.refs_2_.refs_3_, ...), custom_call_target="tpu_custom_call" | custom-call | flops 10000000000 | bytes 1 | tf_op jit(solution)/shard_map/pallas_call | solution.py:160
  49.5 0.6 collective-permute-start.13
  50.1 7.9 %collective-permute-start.12 = (f32[256,128]{1,0:T(8,128)S(1)}, f32[256,128]{1,0:T(8,128)S(1)}, u32[]{:S(2)}, u32[]{:S(2)}) collective-permute-start(f32[256,128]{1,0:T(8,128)S(1)} %get-tuple-element.95), channel_id=1, source_target_pairs={{0,252},{1,253},{2,254},{3,255},{4,8},{5,9},{6,10},{7,11},{8,4},{9... | collective-permute-start | bytes 393224 | tf_op jit(solution)/shard_map/ppermute | solution.py:198
  58.0 0.0 collective-permute-done.10
  58.1 0.1 collective-permute-start.14
  58.2 1.3 %shard_map.105 = (f32[128,1024]{1,0:T(8,128)S(1)}, f32[256,128]{1,0:T(8,128)S(1)}) custom-call(bf16[128,1152]{1,0:T(8,128)(2,1)S(1)} %collective-permute-done.8.refs_0_, bf16[128,1152]{1,0:T(8,128)(2,1)S(1)} %collective-permute-done.9.refs_1_, f32[4,1024]{1,0:T(4,128)S(1)} %get-tuple-element.109.refs_6_.refs_2_, ...), custom_call_target="tpu_custom_call" | custom-call | flops 10000000000 | bytes 1 | tf_op jit(solution)/shard_map/pallas_call | solution.py:160
  59.5 1.7 %collective-permute-start.11 = (f32[128,1024]{1,0:T(8,128)S(1)}, f32[128,1024]{1,0:T(8,128)S(1)}, u32[]{:S(2)}, u32[]{:S(2)}) collective-permute-start(f32[128,1024]{1,0:T(8,128)S(1)} %get-tuple-element.91), channel_id=1, source_target_pairs={{0,2},{1,3},{2,0},{3,1},{4,6},{5,7},{6,4},{7,5},{8,10},{9,11},{10,... | collective-permute-start | bytes 1572872 | tf_op jit(solution)/shard_map/ppermute | solution.py:198
  61.2 1.3 %shard_map.104 = (f32[128,1024]{1,0:T(8,128)S(1)}, f32[256,128]{1,0:T(8,128)S(1)}) custom-call(bf16[128,1152]{1,0:T(8,128)(2,1)S(1)} %collective-permute-done.8.refs_0_, bf16[128,1152]{1,0:T(8,128)(2,1)S(1)} %collective-permute-done.9.refs_1_, f32[7,1024]{1,0:T(8,128)S(1)} %get-tuple-element.111.refs_1_.refs_2_, ...), custom_call_target="tpu_custom_call" | custom-call | flops 10000000000 | bytes 1 | tf_op jit(solution)/shard_map/pallas_call | solution.py:160
  62.6 0.1 collective-permute-start.15
  62.7 0.1 collective-permute-done.14
  62.9 0.1 add_bitcast_fusion
  62.9 1.0 %copy.12 = f32[1024,128]{1,0:T(8,128)} copy(f32[1024,128]{0,1:T(8,128)S(1)} %add_bitcast_fusion) | data formatting | bytes 1048576
  63.9 3.9 %collective-permute-done.15 = bf16[256,128]{1,0:T(8,128)(2,1)S(1)} collective-permute-done((bf16[256,128]{1,0:T(8,128)(2,1)S(1)}, bf16[256,128]{1,0:T(8,128)(2,1)S(1)}, u32[]{:S(2)}, u32[]{:S(2)}) %collective-permute-start.15) | collective-permute-done | bytes 65568 | tf_op jit(solution)/shard_map/ppermute | solution.py:198
  67.9 0.7 convert_add_fusion
  (29 shorter events, 0.2 us)
Async XLA Ops:
  0.6 19.2 %collective-permute-start = (bf16[1024,1024]{1,0:T(8,128)(2,1)}, bf16[1024,1024]{1,0:T(8,128)(2,1)}, u32[]{:S(2)}, u32[]{:S(2)}) collective-permute-start(bf16[1024,1024]{1,0:T(8,128)(2,1)} %tq_ref.1), channel_id=1, source_target_pairs={{0,2},{1,3},{2,0},{3,1},{4,6},{5,7},{6,4},{7,5},{8,10},{9,11},{10,... | collective-permute-start | bytes 6291464 | tf_op jit(solution)/shard_map/ppermute | solution.py:198
  4.0 15.9 %collective-permute-start.1 = (bf16[1024,128]{1,0:T(8,128)(2,1)}, bf16[1024,128]{1,0:T(8,128)(2,1)S(1)}, u32[]{:S(2)}, u32[]{:S(2)}) collective-permute-start(bf16[1024,128]{1,0:T(8,128)(2,1)} %refs_6_.1), channel_id=1, source_target_pairs={{0,2},{1,3},{2,0},{3,1},{4,6},{5,7},{6,4},{7,5},{8,10},{9,11},{10,... | collective-permute-start | bytes 786440 | tf_op jit(solution)/shard_map/ppermute | solution.py:198
  6.0 16.4 %copy-start = (bf16[1024,1024]{1,0:T(8,128)(2,1)S(1)}, bf16[1024,1024]{1,0:T(8,128)(2,1)}, u32[]{:S(2)}) copy-start(bf16[1024,1024]{1,0:T(8,128)(2,1)} %tq_ref.1) | copy-start | bytes 6291460
  6.0 16.4 %copy-start.2 = (bf16[1024,128]{1,0:T(8,128)(2,1)S(1)}, bf16[1024,128]{1,0:T(8,128)(2,1)}, u32[]{:S(2)}) copy-start(bf16[1024,128]{1,0:T(8,128)(2,1)} %refs_6_.1) | copy-start | bytes 786436
  6.0 22.1 %collective-permute-start.3 = (bf16[256,1152]{1,0:T(8,128)(2,1)}, bf16[256,1152]{1,0:T(8,128)(2,1)S(1)}, u32[]{:S(2)}, u32[]{:S(2)}) collective-permute-start(bf16[256,1152]{1,0:T(8,128)(2,1)} %shard_map.95), channel_id=1, source_target_pairs={{0,253},{1,252},{2,255},{3,254},{4,9},{5,8},{6,11},{7,10},{8,5},{9... | collective-permute-start | bytes 1769480 | tf_op jit(solution)/shard_map/ppermute | solution.py:198
  16.6 6.6 %collective-permute-start.4 = (f32[8,1024]{1,0:T(8,128)S(1)}, f32[8,1024]{1,0:T(8,128)S(1)}, u32[]{:S(2)}, u32[]{:S(2)}) collective-permute-start(f32[8,1024]{1,0:T(8,128)S(1)} %pad_maximum_fusion.1), channel_id=1, source_target_pairs={{0,2},{1,3},{2,0},{3,1},{4,6},{5,7},{6,4},{7,5},{8,10},{9,11},{10,... | collective-permute-start | bytes 98312 | tf_op jit(solution)/shard_map/ppermute | solution.py:198
  19.8 2.5 %copy-start.1 = (bf16[512,1152]{1,0:T(8,128)(2,1)S(1)}, bf16[512,1152]{1,0:T(8,128)(2,1)}, u32[]{:S(2)}) copy-start(bf16[512,1152]{1,0:T(8,128)(2,1)} %get-tuple-element.63.refs_0_) | copy-start | bytes 3538948
  19.8 3.3 %copy-start.3 = (bf16[256,1152]{1,0:T(8,128)(2,1)S(1)}, bf16[256,1152]{1,0:T(8,128)(2,1)}, u32[]{:S(2)}) copy-start(bf16[256,1152]{1,0:T(8,128)(2,1)} %shard_map.95) | copy-start | bytes 1769476
  22.3 17.4 %collective-permute-start.6 = (bf16[512,1152]{1,0:T(8,128)(2,1)S(1)}, bf16[512,1152]{1,0:T(8,128)(2,1)S(1)}, u32[]{:S(2)}, u32[]{:S(2)}) collective-permute-start(bf16[512,1152]{1,0:T(8,128)(2,1)S(1)} %copy-done.1), channel_id=1, source_target_pairs={{0,250},{1,251},{2,8},{3,9},{4,254},{5,255},{6,12},{7,13},{8,2},{9... | collective-permute-start | bytes 3538952 | tf_op jit(solution)/shard_map/ppermute | solution.py:198
  23.2 20.9 %collective-permute-start.2 = (bf16[256,1152]{1,0:T(8,128)(2,1)S(1)}, bf16[256,1152]{1,0:T(8,128)(2,1)S(1)}, u32[]{:S(2)}, u32[]{:S(2)}) collective-permute-start(bf16[256,1152]{1,0:T(8,128)(2,1)S(1)} %copy-done.3), channel_id=1, source_target_pairs={{0,5},{1,4},{2,7},{3,6},{4,1},{5,0},{6,3},{7,2},{8,13},{9,12},{10,... | collective-permute-start | bytes 1769480 | tf_op jit(solution)/shard_map/ppermute | solution.py:198
  28.1 9.9 %copy-start.4 = (bf16[128,1152]{1,0:T(8,128)(2,1)S(1)}, bf16[128,1152]{1,0:T(8,128)(2,1)}, u32[]{:S(2)}) copy-start(bf16[128,1152]{1,0:T(8,128)(2,1)} %get-tuple-element.77) | copy-start | bytes 884740
  28.1 16.0 %collective-permute-start.5 = (bf16[256,1152]{1,0:T(8,128)(2,1)S(1)}, bf16[256,1152]{1,0:T(8,128)(2,1)S(1)}, u32[]{:S(2)}, u32[]{:S(2)}) collective-permute-start(bf16[256,1152]{1,0:T(8,128)(2,1)S(1)} %collective-permute-done.3.refs_0_), channel_id=1, source_target_pairs={{0,1},{1,0},{2,3},{3,2},{4,5},{5,4},{6,7},{7,6},{8,9},{9,8},{10,11... | collective-permute-start | bytes 1769480 | tf_op jit(solution)/shard_map/ppermute | solution.py:198
  30.8 13.3 %collective-permute-start.7 = (f32[256,128]{1,0:T(8,128)S(1)}, f32[256,128]{1,0:T(8,128)S(1)}, u32[]{:S(2)}, u32[]{:S(2)}) collective-permute-start(f32[256,128]{1,0:T(8,128)S(1)} %get-tuple-element.75), channel_id=1, source_target_pairs={{0,253},{1,252},{2,255},{3,254},{4,9},{5,8},{6,11},{7,10},{8,5},{9... | collective-permute-start | bytes 393224 | tf_op jit(solution)/shard_map/ppermute | solution.py:198
  38.0 20.1 %collective-permute-start.9 = (bf16[128,1152]{1,0:T(8,128)(2,1)S(1)}, bf16[128,1152]{1,0:T(8,128)(2,1)S(1)}, u32[]{:S(2)}, u32[]{:S(2)}) collective-permute-start(bf16[128,1152]{1,0:T(8,128)(2,1)S(1)} %copy-done.4), channel_id=1, source_target_pairs={{0,5},{1,4},{2,7},{3,6},{4,1},{5,0},{6,3},{7,2},{8,13},{9,12},{10,... | collective-permute-start | bytes 884744 | tf_op jit(solution)/shard_map/ppermute | solution.py:198
  41.9 16.1 %collective-permute-start.10 = (f32[512,128]{1,0:T(8,128)S(1)}, f32[512,128]{1,0:T(8,128)S(1)}, u32[]{:S(2)}, u32[]{:S(2)}) collective-permute-start(f32[512,128]{1,0:T(8,128)S(1)} %pad_maximum_fusion), channel_id=1, source_target_pairs={{0,1},{1,0},{2,3},{3,2},{4,5},{5,4},{6,7},{7,6},{8,9},{9,8},{10,11... | collective-permute-start | bytes 786440 | tf_op jit(solution)/shard_map/ppermute | solution.py:198
  44.1 14.0 %collective-permute-start.8 = (bf16[128,1152]{1,0:T(8,128)(2,1)S(1)}, bf16[128,1152]{1,0:T(8,128)(2,1)S(1)}, u32[]{:S(2)}, u32[]{:S(2)}) collective-permute-start(bf16[128,1152]{1,0:T(8,128)(2,1)S(1)} %slice.37), channel_id=1, source_target_pairs={{0,1},{1,0},{2,3},{3,2},{4,5},{5,4},{6,7},{7,6},{8,9},{9,8},{10,11... | collective-permute-start | bytes 884744 | tf_op jit(solution)/shard_map/ppermute | solution.py:198
  49.5 13.2 %collective-permute-start.13 = (f32[256,128]{1,0:T(8,128)S(1)}, f32[256,128]{1,0:T(8,128)S(1)}, u32[]{:S(2)}, u32[]{:S(2)}) collective-permute-start(f32[256,128]{1,0:T(8,128)S(1)} %get-tuple-element.96), channel_id=1, source_target_pairs={{0,5},{1,4},{2,7},{3,6},{4,1},{5,0},{6,3},{7,2},{8,13},{9,12},{10,... | collective-permute-start | bytes 393224 | tf_op jit(solution)/shard_map/ppermute | solution.py:198
  50.1 12.6 %collective-permute-start.12 = (f32[256,128]{1,0:T(8,128)S(1)}, f32[256,128]{1,0:T(8,128)S(1)}, u32[]{:S(2)}, u32[]{:S(2)}) collective-permute-start(f32[256,128]{1,0:T(8,128)S(1)} %get-tuple-element.95), channel_id=1, source_target_pairs={{0,252},{1,253},{2,254},{3,255},{4,8},{5,9},{6,10},{7,11},{8,4},{9... | collective-permute-start | bytes 393224 | tf_op jit(solution)/shard_map/ppermute | solution.py:198
  58.1 4.8 %collective-permute-start.14 = (f32[256,128]{1,0:T(8,128)S(1)}, f32[256,128]{1,0:T(8,128)S(1)}, u32[]{:S(2)}, u32[]{:S(2)}) collective-permute-start(f32[256,128]{1,0:T(8,128)S(1)} %slice_add_fusion), channel_id=1, source_target_pairs={{0,250},{1,251},{2,8},{3,9},{4,254},{5,255},{6,12},{7,13},{8,2},{9... | collective-permute-start | bytes 393224 | tf_op jit(solution)/shard_map/ppermute | solution.py:198
  59.5 3.4 %collective-permute-start.11 = (f32[128,1024]{1,0:T(8,128)S(1)}, f32[128,1024]{1,0:T(8,128)S(1)}, u32[]{:S(2)}, u32[]{:S(2)}) collective-permute-start(f32[128,1024]{1,0:T(8,128)S(1)} %get-tuple-element.91), channel_id=1, source_target_pairs={{0,2},{1,3},{2,0},{3,1},{4,6},{5,7},{6,4},{7,5},{8,10},{9,11},{10,... | collective-permute-start | bytes 1572872 | tf_op jit(solution)/shard_map/ppermute | solution.py:198
  62.6 5.3 %collective-permute-start.15 = (bf16[256,128]{1,0:T(8,128)(2,1)S(1)}, bf16[256,128]{1,0:T(8,128)(2,1)S(1)}, u32[]{:S(2)}, u32[]{:S(2)}) collective-permute-start(bf16[256,128]{1,0:T(8,128)(2,1)S(1)} %add_convert_fusion), channel_id=1, source_target_pairs={{0,4},{1,5},{2,6},{3,7},{4,0},{5,1},{6,2},{7,3},{8,12},{9,13},{10,... | collective-permute-start | bytes 196616 | tf_op jit(solution)/shard_map/ppermute | solution.py:198

commit v4 on v3

--- a/solution.py
+++ b/solution.py
@@ -235,10 +235,10 @@
     next_half = send(diag_half, pair)
     cross_tail = send(tail, cross)
     q, diag_term = visit([diag_half], (2, 3), both, scales, q, cost=long_cost)
-    diag_back = send(diag_term, diag)
+    diag_back = send(diag_term.astype(jnp.bfloat16), diag)
     far_span, q, own_term = stage(far_span, q, own_term)
     q[:1], far_term = visit([far_span], (3,), both[:1], scales, q[:1], cost=long_cost)
-    pair_back = send(jnp.concatenate([own_term[half:], far_term[half:]]), pair)
+    pair_back = send(jnp.concatenate([own_term[half:], far_term[half:]]).astype(jnp.bfloat16), pair)
 
     cross_half, next_half, q, own_term, far_term, diag_back = stage(
         cross_half, next_half, q, own_term, far_term, diag_back
@@ -248,6 +248,7 @@
     next_back = send(next_term, diag_two)
     q, cross_term = visit([cross_half], (1, 2), both, scales, q, cost=long_cost)
     cross_back = send(cross_term, cross)
+    pair_back = pair_back.astype(jnp.float32)
     far_back = send(far_term[:half] + pair_back[half:], far)
 
     cross_head, cross_tail, q, own_term, pair_back = stage(
@@ -258,7 +259,8 @@
     q_back = send(q[1], core)
     q[:1], last_term = visit(rest, (1,), both[:1], scales, q[:1], cost=long_cost)
     last_back = send((last_term + other_term).astype(jnp.bfloat16), two)
-    total = own_term[:half] + pair_back[:half] + diag_back + next_back + cross_back + far_back
+    total = own_term[:half] + pair_back[:half] + next_back + cross_back + far_back
+    total = total + diag_back.astype(jnp.float32)
     q_out, total = stage((q[0] + q_back).T, total)
     return q_out, total + last_back.astype(jnp.float32)
 

time: 68.8 us -> 68.7 us (level)
  waiting for transfers between devices: 8.01 us -> 6.58 us
  starting transfers between devices: 30.8 us -> 32.2 us
    ppermute x16, waiting for transfers between devices: 8.01 us -> 6.58 us  [send(): return lax.ppermute(block, AXES, edges(n_items, move))]
    ppermute x16, starting transfers between devices: 30.8 us -> 32.2 us  [send(): return lax.ppermute(block, AXES, edges(n_items, move))]
  transfers between devices with their start and end apart: 16 -> 16, of which waited for: 5 -> 4; matrix products, arithmetic and copies ran while one was open for 5% -> 5% of each run, Pallas kernels for 36% -> 36%
where the time goes in v4:
time: 68.7 us; the launch traced here: 68.5 us
  starting transfers between devices  32.2 us (47%)
  Pallas kernels  24.9 us (36%)
  waiting for transfers between devices  6.58 us (10%)
  other arithmetic  2.52 us (4%)
  local copies, waits for them, and re-layouts  1.35 us (2%)
  between operations  1.03 us (1%)
    ppermute x16, starting transfers between devices, send(): return lax.ppermute(block, AXES, edges(n_items, move))  32.2 us
    pallas_call x7, Pallas kernels, visit(): pl.pallas_call(functools.partial(visit_kernel, len(pieces), rows, not tot...  17.4 us
    ppermute x16, waiting for transfers between devices, send(): return lax.ppermute(block, AXES, edges(n_items, move))  6.58 us
    pallas_call x2, Pallas kernels, gather(): pl.pallas_call(functools.partial(gather_kernel, [part[:2] for part in par...  4.37 us
    pallas_call x2, Pallas kernels, turn(): pl.pallas_call(turn_kernel, out_shape=tuple((pltpu.VMEM(block.shape[::-1]...  3.12 us
  transfers between devices with their start and end apart: 16, of which 4 were waited for; matrix products, arithmetic and copies ran while one was open for 5% of the time, Pallas kernels for 36%

profile of v4, /device:TPU:1, one launch (start us, length us, event | category | flops | bytes accessed | tf_op | source)
XLA Modules:
  0.0 68.5 jit_solution(2573931302728150002)
XLA Ops:
  0.6 3.3 %collective-permute-start = (bf16[1024,1024]{1,0:T(8,128)(2,1)}, bf16[1024,1024]{1,0:T(8,128)(2,1)}, u32[]{:S(2)}, u32[]{:S(2)}) collective-permute-start(bf16[1024,1024]{1,0:T(8,128)(2,1)} %tq_ref.1), channel_id=1, source_target_pairs={{0,2},{1,3},{2,0},{3,1},{4,6},{5,7},{6,4},{7,5},{8,10},{9,11},{10,... | collective-permute-start | bytes 6291464 | tf_op jit(solution)/shard_map/ppermute | solution.py:198
  4.0 0.1 collective-permute-start.1
  4.1 1.9 %shard_map.95 = bf16[256,1152]{1,0:T(8,128)(2,1)} custom-call(s32[1]{0:T(128)} %bitcast.rep_ref, bf16[512,1024]{1,0:T(8,128)(2,1)} %teacher_ref.3, bf16[512,128]{1,0:T(8,128)(2,1)} %student_ref.3), custom_call_target="tpu_custom_call" | custom-call | flops 1 | bytes 1 | tf_op jit(solution)/shard_map/pallas_call | solution.py:94
  6.0 0.0 copy-start
  6.0 0.0 copy-start.2
  6.0 8.6 %collective-permute-start.3 = (bf16[256,1152]{1,0:T(8,128)(2,1)}, bf16[256,1152]{1,0:T(8,128)(2,1)S(1)}, u32[]{:S(2)}, u32[]{:S(2)}) collective-permute-start(bf16[256,1152]{1,0:T(8,128)(2,1)} %shard_map.95), channel_id=1, source_target_pairs={{0,253},{1,252},{2,255},{3,254},{4,9},{5,8},{6,11},{7,10},{8,5},{9... | collective-permute-start | bytes 1769480 | tf_op jit(solution)/shard_map/ppermute | solution.py:198
  14.6 0.1 stack.27
  14.6 0.1 iota_compare_fusion.1
  14.7 0.7 %broadcast_compare_fusion = pred[16,7]{0,1:T(8,128)(4,1)S(1)} fusion(s32[16,7]{0,1:T(8,128)} %param.12), kind=kLoop, calls=%fused_computation.18 | loop fusion | flops 112 | bytes 560 | tf_op jit(solution)/shard_map/ne | solution.py:220
  15.4 0.1 and_reduce_fusion
  15.5 0.1 broadcast_in_dim.31
  15.6 0.1 reshape.101
  15.7 0.8 %select_reduce_fusion = (f32[1024]{0:T(1024)S(1)}, f32[1024]{0:T(1024)S(1)}) fusion(f32[4,1024]{1,0:T(4,128)} %param.15, s32[1024]{0:T(1024)} %param.13, f32[4,1024]{1,0:T(4,128)} %param.14), kind=kLoop, calls=%fused_computation.11 | loop fusion | flops 18432 | bytes 45056 | tf_op jit(solution)/shard_map/reduce_sum | solution.py:214
  16.6 0.8 %collective-permute-start.4 = (f32[8,1024]{1,0:T(8,128)S(1)}, f32[8,1024]{1,0:T(8,128)S(1)}, u32[]{:S(2)}, u32[]{:S(2)}) collective-permute-start(f32[8,1024]{1,0:T(8,128)S(1)} %pad_maximum_fusion.1), channel_id=1, source_target_pairs={{0,2},{1,3},{2,0},{3,1},{4,6},{5,7},{6,4},{7,5},{8,10},{9,11},{10,... | collective-permute-start | bytes 98312 | tf_op jit(solution)/shard_map/ppermute | solution.py:198
  17.3 2.5 %shard_map.96 = (bf16[512,1152]{1,0:T(8,128)(2,1)}, bf16[128,1152]{1,0:T(8,128)(2,1)}) custom-call(s32[1]{0:T(128)} %bitcast.rep_ref, bf16[512,1024]{1,0:T(8,128)(2,1)} %teacher_ref.3, bf16[512,128]{1,0:T(8,128)(2,1)} %student_ref.3), custom_call_target="tpu_custom_call" | custom-call | flops 1 | bytes 1 | tf_op jit(solution)/shard_map/pallas_call | solution.py:94
  19.8 0.0 collective-permute-done.1.sq_ref.refs_10_.refs_6_
  19.9 0.0 collective-permute-done.tq_ref
  19.9 2.4 %shard_map.97 = (bf16[1024,1024]{1,0:T(8,128)(2,1)S(1)}, bf16[128,1024]{1,0:T(8,128)(2,1)S(1)}) custom-call(bf16[1024,1024]{1,0:T(8,128)(2,1)} %collective-permute-done.tq_ref, bf16[1024,128]{1,0:T(8,128)(2,1)S(1)} %collective-permute-done.1.sq_ref.refs_10_.refs_6_), custom_call_target="tpu_custom_call" | custom-call | flops 1 | bytes 1 | tf_op jit(solution)/shard_map/pallas_call | solution.py:114
  22.3 0.1 collective-permute-start.6
  22.4 0.7 %shard_map.98 = (bf16[1024,1024]{1,0:T(8,128)(2,1)S(1)}, bf16[128,1024]{1,0:T(8,128)(2,1)S(1)}) custom-call(bf16[1024,1024]{1,0:T(8,128)(2,1)S(1)} %copy-done, bf16[1024,128]{1,0:T(8,128)(2,1)S(1)} %copy-done.2), custom_call_target="tpu_custom_call" | custom-call | flops 1 | bytes 1 | tf_op jit(solution)/shard_map/pallas_call | solution.py:114
  23.1 0.0 collective-permute-done.4
  23.2 0.1 collective-permute-start.2
  23.3 4.7 %shard_map.99 = (f32[128,1024]{1,0:T(8,128)S(1)}, f32[128,1024]{1,0:T(8,128)S(1)}, f32[512,128]{1,0:T(8,128)S(1)}) custom-call(bf16[512,1152]{1,0:T(8,128)(2,1)S(1)} %copy-done.1, f32[7,1024]{1,0:T(8,128)S(1)} %get-tuple-element.111.refs_1_.refs_2_, f32[7,1024]{1,0:T(8,128)S(1)} %get-tuple-element.110.refs_2_.refs_3_, ...), custom_call_target="tpu_custom_call" | custom-call | flops 1 | bytes 1 | tf_op jit(solution)/shard_map/pallas_call | solution.py:160
  28.0 0.2 collective-permute-done.3.refs_0_
  28.1 2.6 %shard_map.100 = (f32[128,1024]{1,0:T(8,128)S(1)}, f32[128,1024]{1,0:T(8,128)S(1)}, f32[256,128]{1,0:T(8,128)S(1)}) custom-call(bf16[256,1152]{1,0:T(8,128)(2,1)S(1)} %collective-permute-done.3.refs_0_, f32[7,1024]{1,0:T(8,128)S(1)} %get-tuple-element.111.refs_1_.refs_2_, f32[7,1024]{1,0:T(8,128)S(1)} %get-tuple-element.110.refs_2_.refs_3_, ...), custom_call_target="tpu_custom_call" | custom-call | flops 10000000000 | bytes 1 | tf_op jit(solution)/shard_map/pallas_call | solution.py:160
  30.8 7.3 %collective-permute-start.7 = (bf16[256,128]{1,0:T(8,128)(2,1)S(1)}, bf16[256,128]{1,0:T(8,128)(2,1)S(1)}, u32[]{:S(2)}, u32[]{:S(2)}) collective-permute-start(bf16[256,128]{1,0:T(8,128)(2,1)S(1)} %convert_element_type.17), channel_id=1, source_target_pairs={{0,253},{1,252},{2,255},{3,254},{4,9},{5,8},{6,11},{7,10},{8,5},{9... | collective-permute-start | bytes 196616 | tf_op jit(solution)/shard_map/ppermute | solution.py:198
  38.0 1.0 %collective-permute-done.6.refs_0_ = bf16[512,1152]{1,0:T(8,128)(2,1)S(1)} collective-permute-done((bf16[512,1152]{1,0:T(8,128)(2,1)S(1)}, bf16[512,1152]{1,0:T(8,128)(2,1)S(1)}, u32[]{:S(2)}, u32[]{:S(2)}) %collective-permute-start.6) | collective-permute-done | bytes 1179680 | tf_op jit(solution)/shard_map/ppermute | solution.py:198
  39.0 2.2 %shard_map.101 = (f32[128,1024]{1,0:T(8,128)S(1)}, f32[512,128]{1,0:T(8,128)S(1)}) custom-call(bf16[512,1152]{1,0:T(8,128)(2,1)S(1)} %collective-permute-done.6.refs_0_, f32[7,1024]{1,0:T(8,128)S(1)} %get-tuple-element.111.refs_1_.refs_2_, f32[7,1024]{1,0:T(8,128)S(1)} %get-tuple-element.110.refs_2_.refs_3_, ...), custom_call_target="tpu_custom_call" | custom-call | flops 10000000000 | bytes 1 | tf_op jit(solution)/shard_map/pallas_call | solution.py:160
  41.2 0.1 collective-permute-start.10
  41.3 1.4 %collective-permute-done.7 = bf16[256,128]{1,0:T(8,128)(2,1)S(1)} collective-permute-done((bf16[256,128]{1,0:T(8,128)(2,1)S(1)}, bf16[256,128]{1,0:T(8,128)(2,1)S(1)}, u32[]{:S(2)}, u32[]{:S(2)}) %collective-permute-start.7) | collective-permute-done | bytes 65568 | tf_op jit(solution)/shard_map/ppermute | solution.py:198
  42.7 0.2 collective-permute-start.8
  42.9 2.6 %shard_map.102 = (f32[128,1024]{1,0:T(8,128)S(1)}, f32[128,1024]{1,0:T(8,128)S(1)}, f32[256,128]{1,0:T(8,128)S(1)}) custom-call(bf16[256,1152]{1,0:T(8,128)(2,1)S(1)} %collective-permute-done.5.refs_0_, f32[7,1024]{1,0:T(8,128)S(1)} %get-tuple-element.111.refs_1_.refs_2_, f32[7,1024]{1,0:T(8,128)S(1)} %get-tuple-element.110.refs_2_.refs_3_, ...), custom_call_target="tpu_custom_call" | custom-call | flops 10000000000 | bytes 1 | tf_op jit(solution)/shard_map/pallas_call | solution.py:160
  45.6 2.6 %shard_map.103 = (f32[128,1024]{1,0:T(8,128)S(1)}, f32[128,1024]{1,0:T(8,128)S(1)}, f32[256,128]{1,0:T(8,128)S(1)}) custom-call(bf16[256,1152]{1,0:T(8,128)(2,1)S(1)} %collective-permute-done.2.refs_0_, f32[7,1024]{1,0:T(8,128)S(1)} %get-tuple-element.111.refs_1_.refs_2_, f32[7,1024]{1,0:T(8,128)S(1)} %get-tuple-element.110.refs_2_.refs_3_, ...), custom_call_target="tpu_custom_call" | custom-call | flops 10000000000 | bytes 1 | tf_op jit(solution)/shard_map/pallas_call | solution.py:160
  48.2 1.9 %collective-permute-start.13 = (f32[256,128]{1,0:T(8,128)S(1)}, f32[256,128]{1,0:T(8,128)S(1)}, u32[]{:S(2)}, u32[]{:S(2)}) collective-permute-start(f32[256,128]{1,0:T(8,128)S(1)} %get-tuple-element.95), channel_id=1, source_target_pairs={{0,5},{1,4},{2,7},{3,6},{4,1},{5,0},{6,3},{7,2},{8,13},{9,12},{10,... | collective-permute-start | bytes 393224 | tf_op jit(solution)/shard_map/ppermute | solution.py:198
  50.1 7.2 %collective-permute-start.12 = (f32[256,128]{1,0:T(8,128)S(1)}, f32[256,128]{1,0:T(8,128)S(1)}, u32[]{:S(2)}, u32[]{:S(2)}) collective-permute-start(f32[256,128]{1,0:T(8,128)S(1)} %get-tuple-element.94), channel_id=1, source_target_pairs={{0,252},{1,253},{2,254},{3,255},{4,8},{5,9},{6,10},{7,11},{8,4},{9... | collective-permute-start | bytes 393224 | tf_op jit(solution)/shard_map/ppermute | solution.py:198
  57.3 0.0 collective-permute-done.10
  57.4 0.1 collective-permute-start.14
  57.5 0.0 collective-permute-done.8.refs_0_
  57.5 1.3 %shard_map.105 = (f32[128,1024]{1,0:T(8,128)S(1)}, f32[256,128]{1,0:T(8,128)S(1)}) custom-call(bf16[128,1152]{1,0:T(8,128)(2,1)S(1)} %collective-permute-done.8.refs_0_, bf16[128,1152]{1,0:T(8,128)(2,1)S(1)} %collective-permute-done.9.refs_1_, f32[4,1024]{1,0:T(4,128)S(1)} %get-tuple-element.109.refs_6_.refs_2_, ...), custom_call_target="tpu_custom_call" | custom-call | flops 10000000000 | bytes 1 | tf_op jit(solution)/shard_map/pallas_call | solution.py:160
  58.8 2.3 %collective-permute-start.11 = (f32[128,1024]{1,0:T(8,128)S(1)}, f32[128,1024]{1,0:T(8,128)S(1)}, u32[]{:S(2)}, u32[]{:S(2)}) collective-permute-start(f32[128,1024]{1,0:T(8,128)S(1)} %get-tuple-element.91), channel_id=1, source_target_pairs={{0,2},{1,3},{2,0},{3,1},{4,6},{5,7},{6,4},{7,5},{8,10},{9,11},{10,... | collective-permute-start | bytes 1572872 | tf_op jit(solution)/shard_map/ppermute | solution.py:198
  61.2 1.3 %shard_map.104 = (f32[128,1024]{1,0:T(8,128)S(1)}, f32[256,128]{1,0:T(8,128)S(1)}) custom-call(bf16[128,1152]{1,0:T(8,128)(2,1)S(1)} %collective-permute-done.8.refs_0_, bf16[128,1152]{1,0:T(8,128)(2,1)S(1)} %collective-permute-done.9.refs_1_, f32[7,1024]{1,0:T(8,128)S(1)} %get-tuple-element.111.refs_1_.refs_2_, ...), custom_call_target="tpu_custom_call" | custom-call | flops 10000000000 | bytes 1 | tf_op jit(solution)/shard_map/pallas_call | solution.py:160
  62.6 0.1 collective-permute-start.15
  62.7 0.0 collective-permute-done.13
  62.7 0.0 collective-permute-done.12
  62.7 0.1 add_bitcast_fusion
  62.8 1.0 %copy.12 = f32[1024,128]{1,0:T(8,128)} copy(f32[1024,128]{0,1:T(8,128)S(1)} %add_bitcast_fusion) | data formatting | bytes 1048576
  63.8 4.0 %collective-permute-done.15 = bf16[256,128]{1,0:T(8,128)(2,1)S(1)} collective-permute-done((bf16[256,128]{1,0:T(8,128)(2,1)S(1)}, bf16[256,128]{1,0:T(8,128)(2,1)S(1)}, u32[]{:S(2)}, u32[]{:S(2)}) %collective-permute-start.15) | collective-permute-done | bytes 65568 | tf_op jit(solution)/shard_map/ppermute | solution.py:198
  67.8 0.7 convert_add_fusion
  (31 shorter events, 0.2 us)
Async XLA Ops:
  0.6 19.2 %collective-permute-start = (bf16[1024,1024]{1,0:T(8,128)(2,1)}, bf16[1024,1024]{1,0:T(8,128)(2,1)}, u32[]{:S(2)}, u32[]{:S(2)}) collective-permute-start(bf16[1024,1024]{1,0:T(8,128)(2,1)} %tq_ref.1), channel_id=1, source_target_pairs={{0,2},{1,3},{2,0},{3,1},{4,6},{5,7},{6,4},{7,5},{8,10},{9,11},{10,... | collective-permute-start | bytes 6291464 | tf_op jit(solution)/shard_map/ppermute | solution.py:198
  4.0 15.9 %collective-permute-start.1 = (bf16[1024,128]{1,0:T(8,128)(2,1)}, bf16[1024,128]{1,0:T(8,128)(2,1)S(1)}, u32[]{:S(2)}, u32[]{:S(2)}) collective-permute-start(bf16[1024,128]{1,0:T(8,128)(2,1)} %refs_6_.1), channel_id=1, source_target_pairs={{0,2},{1,3},{2,0},{3,1},{4,6},{5,7},{6,4},{7,5},{8,10},{9,11},{10,... | collective-permute-start | bytes 786440 | tf_op jit(solution)/shard_map/ppermute | solution.py:198
  6.0 16.4 %copy-start = (bf16[1024,1024]{1,0:T(8,128)(2,1)S(1)}, bf16[1024,1024]{1,0:T(8,128)(2,1)}, u32[]{:S(2)}) copy-start(bf16[1024,1024]{1,0:T(8,128)(2,1)} %tq_ref.1) | copy-start | bytes 6291460
  6.0 16.4 %copy-start.2 = (bf16[1024,128]{1,0:T(8,128)(2,1)S(1)}, bf16[1024,128]{1,0:T(8,128)(2,1)}, u32[]{:S(2)}) copy-start(bf16[1024,128]{1,0:T(8,128)(2,1)} %refs_6_.1) | copy-start | bytes 786436
  6.0 22.1 %collective-permute-start.3 = (bf16[256,1152]{1,0:T(8,128)(2,1)}, bf16[256,1152]{1,0:T(8,128)(2,1)S(1)}, u32[]{:S(2)}, u32[]{:S(2)}) collective-permute-start(bf16[256,1152]{1,0:T(8,128)(2,1)} %shard_map.95), channel_id=1, source_target_pairs={{0,253},{1,252},{2,255},{3,254},{4,9},{5,8},{6,11},{7,10},{8,5},{9... | collective-permute-start | bytes 1769480 | tf_op jit(solution)/shard_map/ppermute | solution.py:198
  16.6 6.6 %collective-permute-start.4 = (f32[8,1024]{1,0:T(8,128)S(1)}, f32[8,1024]{1,0:T(8,128)S(1)}, u32[]{:S(2)}, u32[]{:S(2)}) collective-permute-start(f32[8,1024]{1,0:T(8,128)S(1)} %pad_maximum_fusion.1), channel_id=1, source_target_pairs={{0,2},{1,3},{2,0},{3,1},{4,6},{5,7},{6,4},{7,5},{8,10},{9,11},{10,... | collective-permute-start | bytes 98312 | tf_op jit(solution)/shard_map/ppermute | solution.py:198
  19.8 2.5 %copy-start.1 = (bf16[512,1152]{1,0:T(8,128)(2,1)S(1)}, bf16[512,1152]{1,0:T(8,128)(2,1)}, u32[]{:S(2)}) copy-start(bf16[512,1152]{1,0:T(8,128)(2,1)} %get-tuple-element.63.refs_0_) | copy-start | bytes 3538948
  19.8 3.3 %copy-start.3 = (bf16[256,1152]{1,0:T(8,128)(2,1)S(1)}, bf16[256,1152]{1,0:T(8,128)(2,1)}, u32[]{:S(2)}) copy-start(bf16[256,1152]{1,0:T(8,128)(2,1)} %shard_map.95) | copy-start | bytes 1769476
  22.3 16.7 %collective-permute-start.6 = (bf16[512,1152]{1,0:T(8,128)(2,1)S(1)}, bf16[512,1152]{1,0:T(8,128)(2,1)S(1)}, u32[]{:S(2)}, u32[]{:S(2)}) collective-permute-start(bf16[512,1152]{1,0:T(8,128)(2,1)S(1)} %copy-done.1), channel_id=1, source_target_pairs={{0,250},{1,251},{2,8},{3,9},{4,254},{5,255},{6,12},{7,13},{8,2},{9... | collective-permute-start | bytes 3538952 | tf_op jit(solution)/shard_map/ppermute | solution.py:198
  23.2 19.5 %collective-permute-start.2 = (bf16[256,1152]{1,0:T(8,128)(2,1)S(1)}, bf16[256,1152]{1,0:T(8,128)(2,1)S(1)}, u32[]{:S(2)}, u32[]{:S(2)}) collective-permute-start(bf16[256,1152]{1,0:T(8,128)(2,1)S(1)} %copy-done.3), channel_id=1, source_target_pairs={{0,5},{1,4},{2,7},{3,6},{4,1},{5,0},{6,3},{7,2},{8,13},{9,12},{10,... | collective-permute-start | bytes 1769480 | tf_op jit(solution)/shard_map/ppermute | solution.py:198
  28.1 9.9 %copy-start.4 = (bf16[128,1152]{1,0:T(8,128)(2,1)S(1)}, bf16[128,1152]{1,0:T(8,128)(2,1)}, u32[]{:S(2)}) copy-start(bf16[128,1152]{1,0:T(8,128)(2,1)} %get-tuple-element.77) | copy-start | bytes 884740
  28.1 14.6 %collective-permute-start.5 = (bf16[256,1152]{1,0:T(8,128)(2,1)S(1)}, bf16[256,1152]{1,0:T(8,128)(2,1)S(1)}, u32[]{:S(2)}, u32[]{:S(2)}) collective-permute-start(bf16[256,1152]{1,0:T(8,128)(2,1)S(1)} %collective-permute-done.3.refs_0_), channel_id=1, source_target_pairs={{0,1},{1,0},{2,3},{3,2},{4,5},{5,4},{6,7},{7,6},{8,9},{9,8},{10,11... | collective-permute-start | bytes 1769480 | tf_op jit(solution)/shard_map/ppermute | solution.py:198
  30.8 11.9 %collective-permute-start.7 = (bf16[256,128]{1,0:T(8,128)(2,1)S(1)}, bf16[256,128]{1,0:T(8,128)(2,1)S(1)}, u32[]{:S(2)}, u32[]{:S(2)}) collective-permute-start(bf16[256,128]{1,0:T(8,128)(2,1)S(1)} %convert_element_type.17), channel_id=1, source_target_pairs={{0,253},{1,252},{2,255},{3,254},{4,9},{5,8},{6,11},{7,10},{8,5},{9... | collective-permute-start | bytes 196616 | tf_op jit(solution)/shard_map/ppermute | solution.py:198
  38.0 19.4 %collective-permute-start.9 = (bf16[128,1152]{1,0:T(8,128)(2,1)S(1)}, bf16[128,1152]{1,0:T(8,128)(2,1)S(1)}, u32[]{:S(2)}, u32[]{:S(2)}) collective-permute-start(bf16[128,1152]{1,0:T(8,128)(2,1)S(1)} %copy-done.4), channel_id=1, source_target_pairs={{0,5},{1,4},{2,7},{3,6},{4,1},{5,0},{6,3},{7,2},{8,13},{9,12},{10,... | collective-permute-start | bytes 884744 | tf_op jit(solution)/shard_map/ppermute | solution.py:198
  41.2 16.1 %collective-permute-start.10 = (bf16[512,128]{1,0:T(8,128)(2,1)S(1)}, bf16[512,128]{1,0:T(8,128)(2,1)S(1)}, u32[]{:S(2)}, u32[]{:S(2)}) collective-permute-start(bf16[512,128]{1,0:T(8,128)(2,1)S(1)} %pad_maximum_fusion), channel_id=1, source_target_pairs={{0,1},{1,0},{2,3},{3,2},{4,5},{5,4},{6,7},{7,6},{8,9},{9,8},{10,11... | collective-permute-start | bytes 393224 | tf_op jit(solution)/shard_map/ppermute | solution.py:198
  42.7 14.8 %collective-permute-start.8 = (bf16[128,1152]{1,0:T(8,128)(2,1)S(1)}, bf16[128,1152]{1,0:T(8,128)(2,1)S(1)}, u32[]{:S(2)}, u32[]{:S(2)}) collective-permute-start(bf16[128,1152]{1,0:T(8,128)(2,1)S(1)} %slice.39), channel_id=1, source_target_pairs={{0,1},{1,0},{2,3},{3,2},{4,5},{5,4},{6,7},{7,6},{8,9},{9,8},{10,11... | collective-permute-start | bytes 884744 | tf_op jit(solution)/shard_map/ppermute | solution.py:198
  48.2 14.5 %collective-permute-start.13 = (f32[256,128]{1,0:T(8,128)S(1)}, f32[256,128]{1,0:T(8,128)S(1)}, u32[]{:S(2)}, u32[]{:S(2)}) collective-permute-start(f32[256,128]{1,0:T(8,128)S(1)} %get-tuple-element.95), channel_id=1, source_target_pairs={{0,5},{1,4},{2,7},{3,6},{4,1},{5,0},{6,3},{7,2},{8,13},{9,12},{10,... | collective-permute-start | bytes 393224 | tf_op jit(solution)/shard_map/ppermute | solution.py:198
  50.1 12.5 %collective-permute-start.12 = (f32[256,128]{1,0:T(8,128)S(1)}, f32[256,128]{1,0:T(8,128)S(1)}, u32[]{:S(2)}, u32[]{:S(2)}) collective-permute-start(f32[256,128]{1,0:T(8,128)S(1)} %get-tuple-element.94), channel_id=1, source_target_pairs={{0,252},{1,253},{2,254},{3,255},{4,8},{5,9},{6,10},{7,11},{8,4},{9... | collective-permute-start | bytes 393224 | tf_op jit(solution)/shard_map/ppermute | solution.py:198
  57.4 5.3 %collective-permute-start.14 = (f32[256,128]{1,0:T(8,128)S(1)}, f32[256,128]{1,0:T(8,128)S(1)}, u32[]{:S(2)}, u32[]{:S(2)}) collective-permute-start(f32[256,128]{1,0:T(8,128)S(1)} %slice_add_fusion), channel_id=1, source_target_pairs={{0,250},{1,251},{2,8},{3,9},{4,254},{5,255},{6,12},{7,13},{8,2},{9... | collective-permute-start | bytes 393224 | tf_op jit(solution)/shard_map/ppermute | solution.py:198
  58.8 3.9 %collective-permute-start.11 = (f32[128,1024]{1,0:T(8,128)S(1)}, f32[128,1024]{1,0:T(8,128)S(1)}, u32[]{:S(2)}, u32[]{:S(2)}) collective-permute-start(f32[128,1024]{1,0:T(8,128)S(1)} %get-tuple-element.91), channel_id=1, source_target_pairs={{0,2},{1,3},{2,0},{3,1},{4,6},{5,7},{6,4},{7,5},{8,10},{9,11},{10,... | collective-permute-start | bytes 1572872 | tf_op jit(solution)/shard_map/ppermute | solution.py:198
  62.6 5.3 %collective-permute-start.15 = (bf16[256,128]{1,0:T(8,128)(2,1)S(1)}, bf16[256,128]{1,0:T(8,128)(2,1)S(1)}, u32[]{:S(2)}, u32[]{:S(2)}) collective-permute-start(bf16[256,128]{1,0:T(8,128)(2,1)S(1)} %add_convert_fusion), channel_id=1, source_target_pairs={{0,4},{1,5},{2,6},{3,7},{4,0},{5,1},{6,2},{7,3},{8,12},{9,13},{10,... | collective-permute-start | bytes 196616 | tf_op jit(solution)/shard_map/ppermute | solution.py:198
